TPU v7x, 256 devices: a whole 4x4x8 slice. The times are simulated.
256 devices in a mesh: rows: 16 (over x, z_hi), cols: 16 (over z_lo, y, core).
Axes of the slice: x: 4, y: 4, z: 8 (z_hi: 4, z_lo: 2; z = z_hi * 2 + z_lo), core: 2. Of those that a mesh axis runs over, the one named last changes fastest.
Arguments:
- rainfall: float32 [256, 256], P(('rows', 'cols')), may hold values from 2 to 60
- infil_rate: float32 [256, 256], P(('rows', 'cols')), may hold values from 5 to 80
- porosity: float32 [256, 256], P(('rows', 'cols')), may hold values from 0.38 to 0.5
- soil_liquid: float32 [4, 256, 256], P(None, ('rows', 'cols')), may hold values from 0.1 to 0.3
- soil_ice: float32 [4, 256, 256], P(None, ('rows', 'cols')), may hold values from 0 to 0.15
- flow_dir: int32 [2560, 2560], P('rows', 'cols'), may hold values from 0 to 7
- routing_class: int32 [2560, 2560], P('rows', 'cols'), may hold values from 0 to 2, as said below
- overland_rate: bfloat16 [2560, 2560], P('rows', 'cols'), may hold values from 0.049804688 to 0.44921875
- lateral_rate: bfloat16 [2560, 2560], P('rows', 'cols'), may hold values from 0.049804688 to 0.5
- subgrid_weight: bfloat16 [2560, 2560], P('rows', 'cols'), may hold values from 0.29882812 to 3
Outputs:
- new_liquid: float32 [4, 256, 256], P(None, ('rows', 'cols'))
- ponded: float32 [256, 256], P(('rows', 'cols'))
- channel_water: float32 [256, 256], P(('rows', 'cols'))
Inputs may be any that keep to these rules, and one draw needn't show every extreme that they name: `routing_class`: 0 marks land, 1 channel, 2 lake.
All inputs are finite; a program needn't handle non-finite values.
Results may differ from a plain program's by a relative error of at most 0.0003.
Values sent between devices are 32-bit elements; how exact they have to be, the bound alone decides.
A program may use at most 64 MiB of HBM per device.

v0:
```python
import jax
import jax.numpy as jnp
from jax import lax
from jax.sharding import PartitionSpec as P

REFINE = 10
LAYERS = 4
NSUB = 3


thickness = (0.1, 0.3, 0.6, 1.0)
layer_speed = (1.0, 0.8, 0.6, 0.4)
steps_d8 = ((0, 1), (1, 1), (1, 0), (1, -1), (0, -1), (-1, -1), (-1, 0), (-1, 1))


def extended(cells, sides, width):
    for axis, dim in sides:
        count = lax.axis_size(axis)
        ends = count - 1
        head = lax.slice_in_dim(cells, 0, width, axis=dim)
        tail = lax.slice_in_dim(cells, cells.shape[dim] - width, cells.shape[dim], axis=dim)
        cells = jnp.concatenate(
            [
                lax.ppermute(tail, axis, [(i, (i + 1) % count) for i in range(ends)]),
                cells,
                lax.ppermute(head, axis, [((i + 1) % count, i) for i in range(ends)]),
            ],
            axis=dim,
        )
    return cells


def expand_coarse(coarse):
    lead = coarse.shape[:-2]
    nrow, ncol = coarse.shape[-2:]
    grown = jnp.broadcast_to(coarse[..., :, None, :, None], lead + (nrow, REFINE, ncol, REFINE))
    return grown.reshape(lead + (nrow * REFINE, ncol * REFINE))


def block_mean(fine):
    lead = fine.shape[:-2]
    nrow, ncol = fine.shape[-2:]
    split = fine.reshape(lead + (nrow // REFINE, REFINE, ncol // REFINE, REFINE))
    return jnp.mean(split, axis=(-3, -1))


def infiltrate(rainfall, infil_rate, porosity, soil_liquid, soil_ice):
    top_sat = (soil_liquid[0] + soil_ice[0]) / porosity
    capacity = infil_rate * jnp.maximum(1.0 - top_sat, 0.1)
    excess = rainfall * rainfall / (rainfall + capacity)
    top = soil_liquid[0] + (rainfall - excess) / (1000.0 * thickness[0])
    return (excess, jnp.concatenate([top[None], soil_liquid[1:]], 0))


def outflow_volumes(
    ponded_depth,
    liquid_water,
    frozen_water,
    inverse_porosity,
    overland_flux_rate,
    lateral_flux_rate,
    cell_kind,
):
    q_raw = overland_flux_rate * ponded_depth * ponded_depth / (ponded_depth + 2.0)
    discharge_out = jnp.where(cell_kind == 2, 0.0, q_raw)
    routed = jnp.where(cell_kind == 0, discharge_out, 0.0)
    channel_flags = jnp.where(cell_kind == 1, discharge_out, 0.0)
    speed = jnp.array(layer_speed, jnp.float32)[:, None, None]
    saturation = jnp.minimum((liquid_water + frozen_water) * inverse_porosity, 1.0)
    lateral_flux = lateral_flux_rate * speed * liquid_water * saturation * saturation
    return (discharge_out, jnp.concatenate([routed[None], lateral_flux], 0), channel_flags)


def gather_inflow(moving_water, dirs):
    nrow = moving_water.shape[-2] - 2
    ncol = moving_water.shape[-1] - 2
    total = jnp.zeros(moving_water.shape[:-2] + (nrow, ncol), jnp.float32)
    for code, (d_row, d_col) in enumerate(steps_d8):
        sent = jnp.where(dirs == code, moving_water, 0.0)
        total = total + sent[:, 1 - d_row : 1 - d_row + nrow, 1 - d_col : 1 - d_col + ncol]
    return total


def settle_water(
    ponded_depth,
    liquid_water,
    frozen_water,
    pore_fraction,
    discharge_out,
    lateral_flux,
    inflow_volume,
):
    depth_new = ponded_depth - discharge_out + inflow_volume[0]
    updated_liquid = liquid_water - lateral_flux + inflow_volume[1:]
    spill_volume = jnp.maximum(updated_liquid + frozen_water - pore_fraction, 0.0)
    layer_mm = 1000.0 * jnp.array(thickness, jnp.float32)[:, None, None]
    return (depth_new + jnp.sum(spill_volume * layer_mm, 0), updated_liquid - spill_volume)


def body(
    rainfall,
    infil_rate,
    porosity,
    soil_liquid,
    soil_ice,
    flow_dir,
    routing_class,
    overland_rate,
    lateral_rate,
    subgrid_weight,
):
    excess, liquid_c = infiltrate(rainfall, infil_rate, porosity, soil_liquid, soil_ice)
    strip = jnp.concatenate([excess[None], porosity[None], liquid_c, soil_ice], 0)
    tile_cols = strip.shape[2] // lax.axis_size("cols")
    strip_rows = strip.shape[1]
    rows_all = lax.all_gather(strip, "cols", axis=1, tiled=True)
    tile_block = lax.dynamic_slice_in_dim(
        rows_all, lax.axis_index("cols") * tile_cols, tile_cols, 2
    )
    weight = subgrid_weight.astype(jnp.float32)
    ponded_depth = expand_coarse(tile_block[0]) * weight / expand_coarse(block_mean(weight))
    pore_fraction = expand_coarse(tile_block[1])
    liquid_water = expand_coarse(tile_block[2 : 2 + LAYERS])
    frozen_water = expand_coarse(tile_block[2 + LAYERS :])
    inverse_porosity = 1.0 / pore_fraction
    overland_flux_rate = overland_rate.astype(jnp.float32)
    lateral_flux_rate = lateral_rate.astype(jnp.float32)
    channel_total = jnp.zeros(ponded_depth.shape, jnp.float32)
    dirs = extended(flow_dir, (("rows", 0), ("cols", 1)), 1)
    for step in range(NSUB):
        discharge_out, moving_water, channel_flags = outflow_volumes(
            ponded_depth,
            liquid_water,
            frozen_water,
            inverse_porosity,
            overland_flux_rate,
            lateral_flux_rate,
            routing_class,
        )
        padded = extended(moving_water, (("rows", 1), ("cols", 2)), 1)
        inflow_volume = gather_inflow(padded, dirs)
        ponded_depth, liquid_water = settle_water(
            ponded_depth,
            liquid_water,
            frozen_water,
            pore_fraction,
            discharge_out,
            moving_water[1:],
            inflow_volume,
        )
        channel_total = channel_total + channel_flags
    stack_back = jnp.concatenate(
        [block_mean(liquid_water), block_mean(ponded_depth)[None], block_mean(channel_total)[None]],
        0,
    )
    cols_all = lax.all_gather(stack_back, "cols", axis=2, tiled=True)
    back = lax.dynamic_slice_in_dim(cols_all, lax.axis_index("cols") * strip_rows, strip_rows, 1)
    return (back[:LAYERS], back[LAYERS], back[LAYERS + 1])


def solution(mesh):
    return jax.shard_map(
        body,
        mesh=mesh,
        in_specs=(
            P(("rows", "cols"), None),
            P(("rows", "cols"), None),
            P(("rows", "cols"), None),
            P(None, ("rows", "cols"), None),
            P(None, ("rows", "cols"), None),
            P("rows", "cols"),
            P("rows", "cols"),
            P("rows", "cols"),
            P("rows", "cols"),
            P("rows", "cols"),
        ),
        out_specs=(
            P(None, ("rows", "cols"), None),
            P(("rows", "cols"), None),
            P(("rows", "cols"), None),
        ),
        check_vma=False,
    )
```

profile of v0, /device:TPU:6, one launch (start us, length us, event | category | flops | bytes accessed | tf_op | source)
XLA Modules:
  0.0 182.1 jit_solution(2162308386818041069)
XLA Ops:
  1.4 8.5 %collective-permute-start.1 = (s32[1,160]{1,0:T(1,128)S(1)}, s32[1,160]{1,0:T(1,128)S(1)}, u32[]{:S(2)}, u32[]{:S(2)}) collective-permute-start(s32[1,160]{1,0:T(1,128)S(1)} %get-tuple-element.60), channel_id=1, source_target_pairs={{16,0},{32,16},{48,32},{64,48},{80,64},{96,80},{112,96},{128,112},... | collective-permute-start | bytes 1928 | tf_op jit(solution)/shard_map/ppermute | solution.py:26
  9.8 1.9 %collective-permute-start = (s32[1,160]{1,0:T(1,128)S(1)}, s32[1,160]{1,0:T(1,128)S(1)}, u32[]{:S(2)}, u32[]{:S(2)}) collective-permute-start(s32[1,160]{1,0:T(1,128)S(1)} %get-tuple-element.59), channel_id=1, source_target_pairs={{0,16},{16,32},{32,48},{48,64},{64,80},{80,96},{96,112},{112,128},... | collective-permute-start | bytes 1928 | tf_op jit(solution)/shard_map/ppermute | solution.py:24
  14.7 20.1 %all_gather.6 = f32[10,16,256]{2,0,1:T(8,128)S(1)} all-gather(f32[10,1,256]{2,0,1:T(8,128)S(1)} %concatenate.39), channel_id=1, replica_groups=mesh['rows'=16,'cols'=16] {'cols'}, dimensions={1}, use_global_device_ids=true | all-gather | bytes 174080 | tf_op jit(solution)/shard_map/all_gather | solution.py:116
  34.9 2.7 %broadcast_in_dim.149 = f32[4,16,10,16,10]{4,3,2,1,0:T(8,128)} broadcast(f32[4,16,16]{2,1,0:T(8,128)S(1)} %copy.36), dimensions={0,1,3} | broadcast | bytes 413696 | tf_op jit(solution)/shard_map/broadcast_in_dim | solution.py:36
  37.7 4.5 %reshape.95 = f32[4,160,160]{2,1,0:T(8,128)S(1)} reshape(f32[4,16,10,16,10]{4,3,2,1,0:T(8,128)} %broadcast_in_dim.149) | data formatting | bytes 819200 | tf_op jit(solution)/shard_map/reshape | solution.py:37
  43.2 2.7 %broadcast_in_dim.148 = f32[4,16,10,16,10]{4,3,2,1,0:T(8,128)} broadcast(f32[4,16,16]{2,1,0:T(8,128)S(1)} %copy.35), dimensions={0,1,3} | broadcast | bytes 413696 | tf_op jit(solution)/shard_map/broadcast_in_dim | solution.py:36
  45.9 4.5 %reshape.94 = f32[4,160,160]{2,1,0:T(8,128)S(1)} reshape(f32[4,16,10,16,10]{4,3,2,1,0:T(8,128)} %broadcast_in_dim.148) | data formatting | bytes 819200 | tf_op jit(solution)/shard_map/reshape | solution.py:37
  55.6 3.0 %collective-permute-start.2 = (s32[162,1]{1,0:T(8,128)S(1)}, s32[162,1]{1,0:T(8,128)S(1)}, u32[]{:S(2)}, u32[]{:S(2)}) collective-permute-start(s32[162,1]{1,0:T(8,128)S(1)} %get-tuple-element.57), channel_id=1, source_target_pairs={{0,1},{1,2},{2,3},{3,4},{4,5},{5,6},{6,7},{7,8},{8,9},{9,10},{10,1... | collective-permute-start | bytes 1952 | tf_op jit(solution)/shard_map/ppermute | solution.py:24
  58.7 6.9 %collective-permute-start.5 = (f32[5,1,160]{2,1,0:T(1,128)S(1)}, f32[5,1,160]{2,1,0:T(1,128)S(1)}, u32[]{:S(2)}, u32[]{:S(2)}) collective-permute-start(f32[5,1,160]{2,1,0:T(1,128)S(1)} %get-tuple-element.43), channel_id=1, source_target_pairs={{16,0},{32,16},{48,32},{64,48},{80,64},{96,80},{112,96},{128,112},... | collective-permute-start | bytes 9608 | tf_op jit(solution)/shard_map/ppermute | solution.py:26
  65.6 1.9 %collective-permute-start.4 = (f32[5,1,160]{2,1,0:T(1,128)S(1)}, f32[5,1,160]{2,1,0:T(1,128)S(1)}, u32[]{:S(2)}, u32[]{:S(2)}) collective-permute-start(f32[5,1,160]{2,1,0:T(1,128)S(1)} %get-tuple-element.42), channel_id=1, source_target_pairs={{0,16},{16,32},{32,48},{48,64},{64,80},{80,96},{96,112},{112,128},... | collective-permute-start | bytes 9608 | tf_op jit(solution)/shard_map/ppermute | solution.py:24
  67.7 6.4 %collective-permute-done.4 = f32[5,1,160]{2,1,0:T(1,128)S(1)} collective-permute-done((f32[5,1,160]{2,1,0:T(1,128)S(1)}, f32[5,1,160]{2,1,0:T(1,128)S(1)}, u32[]{:S(2)}, u32[]{:S(2)}) %collective-permute-start.4) | collective-permute-done | bytes 3232 | tf_op jit(solution)/shard_map/ppermute | solution.py:24
  75.7 3.1 %collective-permute-start.6 = (f32[5,162,1]{2,1,0:T(8,128)S(1)}, f32[5,162,1]{2,1,0:T(8,128)S(1)}, u32[]{:S(2)}, u32[]{:S(2)}) collective-permute-start(f32[5,162,1]{2,1,0:T(8,128)S(1)} %get-tuple-element.36), channel_id=1, source_target_pairs={{0,1},{1,2},{2,3},{3,4},{4,5},{5,6},{6,7},{7,8},{8,9},{9,10},{10,1... | collective-permute-start | bytes 9728 | tf_op jit(solution)/shard_map/ppermute | solution.py:24
  83.1 1.9 %collective-permute-start.9 = (f32[5,1,160]{2,1,0:T(1,128)S(1)}, f32[5,1,160]{2,1,0:T(1,128)S(1)}, u32[]{:S(2)}, u32[]{:S(2)}) collective-permute-start(f32[5,1,160]{2,1,0:T(1,128)S(1)} %get-tuple-element.41), channel_id=1, source_target_pairs={{16,0},{32,16},{48,32},{64,48},{80,64},{96,80},{112,96},{128,112},... | collective-permute-start | bytes 9608 | tf_op jit(solution)/shard_map/ppermute | solution.py:26
  85.0 5.0 %collective-permute-start.8 = (f32[5,1,160]{2,1,0:T(1,128)S(1)}, f32[5,1,160]{2,1,0:T(1,128)S(1)}, u32[]{:S(2)}, u32[]{:S(2)}) collective-permute-start(f32[5,1,160]{2,1,0:T(1,128)S(1)} %get-tuple-element.40), channel_id=1, source_target_pairs={{0,16},{16,32},{32,48},{48,64},{64,80},{80,96},{96,112},{112,128},... | collective-permute-start | bytes 9608 | tf_op jit(solution)/shard_map/ppermute | solution.py:24
  90.0 3.7 %collective-permute-done.8 = f32[5,1,160]{2,1,0:T(1,128)S(1)} collective-permute-done((f32[5,1,160]{2,1,0:T(1,128)S(1)}, f32[5,1,160]{2,1,0:T(1,128)S(1)}, u32[]{:S(2)}, u32[]{:S(2)}) %collective-permute-start.8) | collective-permute-done | bytes 3232 | tf_op jit(solution)/shard_map/ppermute | solution.py:24
  95.3 6.5 %collective-permute-start.10 = (f32[5,162,1]{2,1,0:T(8,128)S(1)}, f32[5,162,1]{2,1,0:T(8,128)S(1)}, u32[]{:S(2)}, u32[]{:S(2)}) collective-permute-start(f32[5,162,1]{2,1,0:T(8,128)S(1)} %get-tuple-element.34), channel_id=1, source_target_pairs={{0,1},{1,2},{2,3},{3,4},{4,5},{5,6},{6,7},{7,8},{8,9},{9,10},{10,1... | collective-permute-start | bytes 9728 | tf_op jit(solution)/shard_map/ppermute | solution.py:24
  106.2 1.9 %collective-permute-start.13 = (f32[5,1,160]{2,1,0:T(1,128)S(1)}, f32[5,1,160]{2,1,0:T(1,128)S(1)}, u32[]{:S(2)}, u32[]{:S(2)}) collective-permute-start(f32[5,1,160]{2,1,0:T(1,128)S(1)} %get-tuple-element.39), channel_id=1, source_target_pairs={{16,0},{32,16},{48,32},{64,48},{80,64},{96,80},{112,96},{128,112},... | collective-permute-start | bytes 9608 | tf_op jit(solution)/shard_map/ppermute | solution.py:26
  108.2 4.8 %collective-permute-start.12 = (f32[5,1,160]{2,1,0:T(1,128)S(1)}, f32[5,1,160]{2,1,0:T(1,128)S(1)}, u32[]{:S(2)}, u32[]{:S(2)}) collective-permute-start(f32[5,1,160]{2,1,0:T(1,128)S(1)} %get-tuple-element.38), channel_id=1, source_target_pairs={{0,16},{16,32},{32,48},{48,64},{64,80},{80,96},{96,112},{112,128},... | collective-permute-start | bytes 9608 | tf_op jit(solution)/shard_map/ppermute | solution.py:24
  113.0 3.7 %collective-permute-done.12 = f32[5,1,160]{2,1,0:T(1,128)S(1)} collective-permute-done((f32[5,1,160]{2,1,0:T(1,128)S(1)}, f32[5,1,160]{2,1,0:T(1,128)S(1)}, u32[]{:S(2)}, u32[]{:S(2)}) %collective-permute-start.12) | collective-permute-done | bytes 3232 | tf_op jit(solution)/shard_map/ppermute | solution.py:24
  119.1 9.5 %collective-permute-start.14 = (f32[5,162,1]{2,1,0:T(8,128)}, f32[5,162,1]{2,1,0:T(8,128)}, u32[]{:S(2)}, u32[]{:S(2)}) collective-permute-start(f32[5,162,1]{2,1,0:T(8,128)} %get-tuple-element.32), channel_id=1, source_target_pairs={{0,1},{1,2},{2,3},{3,4},{4,5},{5,6},{6,7},{7,8},{8,9},{9,10},{10,1... | collective-permute-start | bytes 9728 | tf_op jit(solution)/shard_map/ppermute | solution.py:24
  136.2 4.6 %reshape.100 = f32[4,16,10,16,10]{4,3,2,1,0:T(8,128)} reshape(f32[4,160,160]{2,1,0:T(8,128)S(1)} %copy-done) | data formatting | bytes 819200 | tf_op jit(solution)/shard_map/reshape | solution.py:43
  140.8 2.9 %reduce_sum.66 = f32[4,16,16]{2,1,0:T(8,128)S(1)} reduce(f32[4,16,10,16,10]{4,3,2,1,0:T(8,128)} %reshape.100, f32[]{:T(128)} %constant.27.clone.1), dimensions={2,4}, to_apply=%region_3.4 | reduce | flops 101376 | bytes 413700 | tf_op jit(solution)/shard_map/reduce_sum | solution.py:44
  143.8 32.7 %all_gather.7 = f32[6,16,256]{1,0,2:T(8,128)S(1)} all-gather(f32[6,16,16]{1,0,2:T(8,128)S(1)} %copy.37), channel_id=1, replica_groups=mesh['rows'=16,'cols'=16] {'cols'}, dimensions={2}, use_global_device_ids=true | all-gather | bytes 104448 | tf_op jit(solution)/shard_map/all_gather | solution.py:156
  177.7 4.4 %dynamic-slice_reduce_fusion = (f32[256]{0:T(256)}, f32[256]{0:T(256)}) fusion(f32[6,16,256]{1,0,2:T(8,128)S(1)} %all_gather.7, s32[]{:T(128)S(6)} %add.204, s32[]{:T(128)S(6)} %select_n.142, s32[]{:T(128)S(6)} %add.203), kind=kLoop, calls=%fused_computation.94 | loop fusion | bytes 4108 | tf_op jit(solution)/shard_map/slice | solution.py:158
  (154 shorter events, 32.6 us)
Async XLA Ops:
  1.4 52.8 %collective-permute-start.1 = (s32[1,160]{1,0:T(1,128)S(1)}, s32[1,160]{1,0:T(1,128)S(1)}, u32[]{:S(2)}, u32[]{:S(2)}) collective-permute-start(s32[1,160]{1,0:T(1,128)S(1)} %get-tuple-element.60), channel_id=1, source_target_pairs={{16,0},{32,16},{48,32},{64,48},{80,64},{96,80},{112,96},{128,112},... | collective-permute-start | bytes 1928 | tf_op jit(solution)/shard_map/ppermute | solution.py:26
  9.8 44.3 %collective-permute-start = (s32[1,160]{1,0:T(1,128)S(1)}, s32[1,160]{1,0:T(1,128)S(1)}, u32[]{:S(2)}, u32[]{:S(2)}) collective-permute-start(s32[1,160]{1,0:T(1,128)S(1)} %get-tuple-element.59), channel_id=1, source_target_pairs={{0,16},{16,32},{32,48},{48,64},{64,80},{80,96},{96,112},{112,128},... | collective-permute-start | bytes 1928 | tf_op jit(solution)/shard_map/ppermute | solution.py:24
  54.1 28.2 %copy-start.1 = (f32[160,160]{1,0:T(8,128)}, f32[160,160]{1,0:T(8,128)S(1)}, u32[]{:S(2)}) copy-start(f32[160,160]{1,0:T(8,128)S(1)} %get-tuple-element.24) | copy-start | bytes 307204
  54.1 51.3 %copy-start.11 = (pred[160,160]{1,0:T(8,128)(4,1)}, pred[160,160]{1,0:T(8,128)(4,1)S(1)}, u32[]{:S(2)}) copy-start(pred[160,160]{1,0:T(8,128)(4,1)S(1)} %get-tuple-element.25) | copy-start | bytes 76804
  54.3 13.2 %collective-permute-start.3 = (s32[162,1]{1,0:T(8,128)S(1)}, s32[162,1]{1,0:T(8,128)S(1)}, u32[]{:S(2)}, u32[]{:S(2)}) collective-permute-start(s32[162,1]{1,0:T(8,128)S(1)} %get-tuple-element.58), channel_id=1, source_target_pairs={{1,0},{2,1},{3,2},{4,3},{5,4},{6,5},{7,6},{8,7},{9,8},{10,9},{11,1... | collective-permute-start | bytes 1952 | tf_op jit(solution)/shard_map/ppermute | solution.py:26
  55.6 11.9 %collective-permute-start.2 = (s32[162,1]{1,0:T(8,128)S(1)}, s32[162,1]{1,0:T(8,128)S(1)}, u32[]{:S(2)}, u32[]{:S(2)}) collective-permute-start(s32[162,1]{1,0:T(8,128)S(1)} %get-tuple-element.57), channel_id=1, source_target_pairs={{0,1},{1,2},{2,3},{3,4},{4,5},{5,6},{6,7},{7,8},{8,9},{9,10},{10,1... | collective-permute-start | bytes 1952 | tf_op jit(solution)/shard_map/ppermute | solution.py:24
  58.7 9.0 %collective-permute-start.5 = (f32[5,1,160]{2,1,0:T(1,128)S(1)}, f32[5,1,160]{2,1,0:T(1,128)S(1)}, u32[]{:S(2)}, u32[]{:S(2)}) collective-permute-start(f32[5,1,160]{2,1,0:T(1,128)S(1)} %get-tuple-element.43), channel_id=1, source_target_pairs={{16,0},{32,16},{48,32},{64,48},{80,64},{96,80},{112,96},{128,112},... | collective-permute-start | bytes 9608 | tf_op jit(solution)/shard_map/ppermute | solution.py:26
  65.6 8.5 %collective-permute-start.4 = (f32[5,1,160]{2,1,0:T(1,128)S(1)}, f32[5,1,160]{2,1,0:T(1,128)S(1)}, u32[]{:S(2)}, u32[]{:S(2)}) collective-permute-start(f32[5,1,160]{2,1,0:T(1,128)S(1)} %get-tuple-element.42), channel_id=1, source_target_pairs={{0,16},{16,32},{32,48},{48,64},{64,80},{80,96},{96,112},{112,128},... | collective-permute-start | bytes 9608 | tf_op jit(solution)/shard_map/ppermute | solution.py:24
  74.4 5.3 %collective-permute-start.7 = (f32[5,162,1]{2,1,0:T(8,128)S(1)}, f32[5,162,1]{2,1,0:T(8,128)S(1)}, u32[]{:S(2)}, u32[]{:S(2)}) collective-permute-start(f32[5,162,1]{2,1,0:T(8,128)S(1)} %get-tuple-element.37), channel_id=1, source_target_pairs={{1,0},{2,1},{3,2},{4,3},{5,4},{6,5},{7,6},{8,7},{9,8},{10,9},{11,1... | collective-permute-start | bytes 9728 | tf_op jit(solution)/shard_map/ppermute | solution.py:26
  75.7 4.4 %collective-permute-start.6 = (f32[5,162,1]{2,1,0:T(8,128)S(1)}, f32[5,162,1]{2,1,0:T(8,128)S(1)}, u32[]{:S(2)}, u32[]{:S(2)}) collective-permute-start(f32[5,162,1]{2,1,0:T(8,128)S(1)} %get-tuple-element.36), channel_id=1, source_target_pairs={{0,1},{1,2},{2,3},{3,4},{4,5},{5,6},{6,7},{7,8},{8,9},{9,10},{10,1... | collective-permute-start | bytes 9728 | tf_op jit(solution)/shard_map/ppermute | solution.py:24
  79.0 24.6 %copy-start.16 = (pred[160,160]{1,0:T(8,128)(4,1)}, pred[160,160]{1,0:T(8,128)(4,1)S(1)}, u32[]{:S(2)}) copy-start(pred[160,160]{1,0:T(8,128)(4,1)S(1)} %slice.243) | copy-start | bytes 76804
  79.1 24.5 %copy-start.18 = (pred[160,160]{1,0:T(8,128)(4,1)}, pred[160,160]{1,0:T(8,128)(4,1)S(1)}, u32[]{:S(2)}) copy-start(pred[160,160]{1,0:T(8,128)(4,1)S(1)} %slice.241) | copy-start | bytes 76804
  79.2 24.4 %copy-start.20 = (pred[160,160]{1,0:T(8,128)(4,1)}, pred[160,160]{1,0:T(8,128)(4,1)S(1)}, u32[]{:S(2)}) copy-start(pred[160,160]{1,0:T(8,128)(4,1)S(1)} %slice.239) | copy-start | bytes 76804
  79.4 24.2 %copy-start.22 = (pred[160,160]{1,0:T(8,128)(4,1)}, pred[160,160]{1,0:T(8,128)(4,1)S(1)}, u32[]{:S(2)}) copy-start(pred[160,160]{1,0:T(8,128)(4,1)S(1)} %slice.237) | copy-start | bytes 76804
  79.5 24.1 %copy-start.24 = (pred[160,160]{1,0:T(8,128)(4,1)}, pred[160,160]{1,0:T(8,128)(4,1)S(1)}, u32[]{:S(2)}) copy-start(pred[160,160]{1,0:T(8,128)(4,1)S(1)} %slice.235) | copy-start | bytes 76804
  79.6 24.0 %copy-start.26 = (pred[160,160]{1,0:T(8,128)(4,1)}, pred[160,160]{1,0:T(8,128)(4,1)S(1)}, u32[]{:S(2)}) copy-start(pred[160,160]{1,0:T(8,128)(4,1)S(1)} %slice.233) | copy-start | bytes 76804
  83.1 6.9 %collective-permute-start.9 = (f32[5,1,160]{2,1,0:T(1,128)S(1)}, f32[5,1,160]{2,1,0:T(1,128)S(1)}, u32[]{:S(2)}, u32[]{:S(2)}) collective-permute-start(f32[5,1,160]{2,1,0:T(1,128)S(1)} %get-tuple-element.41), channel_id=1, source_target_pairs={{16,0},{32,16},{48,32},{64,48},{80,64},{96,80},{112,96},{128,112},... | collective-permute-start | bytes 9608 | tf_op jit(solution)/shard_map/ppermute | solution.py:26
  85.0 8.7 %collective-permute-start.8 = (f32[5,1,160]{2,1,0:T(1,128)S(1)}, f32[5,1,160]{2,1,0:T(1,128)S(1)}, u32[]{:S(2)}, u32[]{:S(2)}) collective-permute-start(f32[5,1,160]{2,1,0:T(1,128)S(1)} %get-tuple-element.40), channel_id=1, source_target_pairs={{0,16},{16,32},{32,48},{48,64},{64,80},{80,96},{96,112},{112,128},... | collective-permute-start | bytes 9608 | tf_op jit(solution)/shard_map/ppermute | solution.py:24
  94.0 7.8 %collective-permute-start.11 = (f32[5,162,1]{2,1,0:T(8,128)S(1)}, f32[5,162,1]{2,1,0:T(8,128)S(1)}, u32[]{:S(2)}, u32[]{:S(2)}) collective-permute-start(f32[5,162,1]{2,1,0:T(8,128)S(1)} %get-tuple-element.35), channel_id=1, source_target_pairs={{1,0},{2,1},{3,2},{4,3},{5,4},{6,5},{7,6},{8,7},{9,8},{10,9},{11,1... | collective-permute-start | bytes 9728 | tf_op jit(solution)/shard_map/ppermute | solution.py:26
  95.3 7.9 %collective-permute-start.10 = (f32[5,162,1]{2,1,0:T(8,128)S(1)}, f32[5,162,1]{2,1,0:T(8,128)S(1)}, u32[]{:S(2)}, u32[]{:S(2)}) collective-permute-start(f32[5,162,1]{2,1,0:T(8,128)S(1)} %get-tuple-element.34), channel_id=1, source_target_pairs={{0,1},{1,2},{2,3},{3,4},{4,5},{5,6},{6,7},{7,8},{8,9},{9,10},{10,1... | collective-permute-start | bytes 9728 | tf_op jit(solution)/shard_map/ppermute | solution.py:24
  106.2 6.8 %collective-permute-start.13 = (f32[5,1,160]{2,1,0:T(1,128)S(1)}, f32[5,1,160]{2,1,0:T(1,128)S(1)}, u32[]{:S(2)}, u32[]{:S(2)}) collective-permute-start(f32[5,1,160]{2,1,0:T(1,128)S(1)} %get-tuple-element.39), channel_id=1, source_target_pairs={{16,0},{32,16},{48,32},{64,48},{80,64},{96,80},{112,96},{128,112},... | collective-permute-start | bytes 9608 | tf_op jit(solution)/shard_map/ppermute | solution.py:26
  108.2 8.5 %collective-permute-start.12 = (f32[5,1,160]{2,1,0:T(1,128)S(1)}, f32[5,1,160]{2,1,0:T(1,128)S(1)}, u32[]{:S(2)}, u32[]{:S(2)}) collective-permute-start(f32[5,1,160]{2,1,0:T(1,128)S(1)} %get-tuple-element.38), channel_id=1, source_target_pairs={{0,16},{16,32},{32,48},{48,64},{64,80},{80,96},{96,112},{112,128},... | collective-permute-start | bytes 9608 | tf_op jit(solution)/shard_map/ppermute | solution.py:24
  117.8 10.8 %collective-permute-start.15 = (f32[5,162,1]{2,1,0:T(8,128)}, f32[5,162,1]{2,1,0:T(8,128)}, u32[]{:S(2)}, u32[]{:S(2)}) collective-permute-start(f32[5,162,1]{2,1,0:T(8,128)} %get-tuple-element.33), channel_id=1, source_target_pairs={{1,0},{2,1},{3,2},{4,3},{5,4},{6,5},{7,6},{8,7},{9,8},{10,9},{11,1... | collective-permute-start | bytes 9728 | tf_op jit(solution)/shard_map/ppermute | solution.py:26
  119.1 10.5 %collective-permute-start.14 = (f32[5,162,1]{2,1,0:T(8,128)}, f32[5,162,1]{2,1,0:T(8,128)}, u32[]{:S(2)}, u32[]{:S(2)}) collective-permute-start(f32[5,162,1]{2,1,0:T(8,128)} %get-tuple-element.32), channel_id=1, source_target_pairs={{0,1},{1,2},{2,3},{3,4},{4,5},{5,6},{6,7},{7,8},{8,9},{9,10},{10,1... | collective-permute-start | bytes 9728 | tf_op jit(solution)/shard_map/ppermute | solution.py:24
  (27 other events, 113.6 us)
where the time goes:
time: 186 us; the launch traced here: 182 us
  starting transfers between devices  60.2 us (32%)
  blocking collectives  52.8 us (28%)
  local copies, waits for them, and re-layouts  36.2 us (19%)
  waiting for transfers between devices  16.5 us (9%)
  other arithmetic  14.8 us (8%)
    ppermute x8, starting transfers between devices, extended(): lax.ppermute(tail, axis, [(i, (i + 1) % count) for i in range(ends)])  35.7 us
    all_gather x1, blocking collectives, body(): cols_all = lax.all_gather(stack_back, 'cols', axis=2, tiled=True)  32.7 us
    ppermute x8, starting transfers between devices, extended(): lax.ppermute(head, axis, [((i + 1) % count, i) for i in range(ends)])  24.4 us
    all_gather x1, blocking collectives, body(): rows_all = lax.all_gather(strip, 'cols', axis=1, tiled=True)  20.1 us
    ppermute x8, waiting for transfers between devices, extended(): lax.ppermute(tail, axis, [(i, (i + 1) % count) for i in range(ends)])  16.5 us
    reshape x5, local copies, waits for them, and re-layouts, expand_coarse(): return grown.reshape(lead + (nrow * REFINE, ncol * REFINE))  10.8 us
    reshape x4, local copies, waits for them, and re-layouts, block_mean(): fine.reshape(lead + (nrow // REFINE, REFINE, ncol // REFINE, REFINE))  6.8 us
    broadcast_in_dim x5, local copies, waits for them, and re-layouts, expand_coarse(): jnp.broadcast_to(coarse[..., :, None, :, None], lead + (nrow, REFINE, nco...  5.94 us
  transfers between devices with their start and end apart: 16, of which 6 were waited for; matrix products, arithmetic and copies ran while one was open for 12% of the time, Pallas kernels for 0%

commit v1 on v0

v1 whole, which is shorter than its diff:
```python
import functools

import jax
import jax.numpy as jnp
from jax import lax
from jax.experimental import pallas as pl
from jax.experimental.pallas import tpu as pltpu
from jax.sharding import PartitionSpec as P

MESH = pl.DeviceIdType.MESH
REFINE = 10
LAYERS = 4
TILE = 160
CR = 16
W = 256
HALO = 3

thickness = (0.1, 0.3, 0.6, 1.0)
layer_speed = (1.0, 0.8, 0.6, 0.4)

DIR, ORATE, KIND, LRATE, SHARE = range(5)
FIELDS = 5
COARSE = 10


def iota(shape, dim):
    return lax.broadcasted_iota(jnp.int32, shape, dim)


def take(x, index):
    return jnp.take_along_axis(x, index, axis=1, mode="promise_in_bounds")


def tenth(x):
    return lax.shift_right_logical(x * 6554, 16)


def split3(x):
    hi = x.astype(jnp.bfloat16)
    r = x - hi.astype(jnp.float32)
    mid = r.astype(jnp.bfloat16)
    lo = (r - mid.astype(jnp.float32)).astype(jnp.bfloat16)
    return jnp.concatenate([hi, mid, lo], 0)


def dot3(x, ones):
    n = x.shape[0]
    y = jnp.dot(split3(x), ones, preferred_element_type=jnp.float32)
    return y[:n] + y[n : 2 * n] + y[2 * n :]


def inflow_masks(d_up, d_mid, d_down):
    return (
        d_up == 1.0,
        d_mid == 0.0,
        d_down == 7.0,
        d_up == 3.0,
        d_mid == 4.0,
        d_down == 5.0,
        d_up == 2.0,
        d_down == 6.0,
    )


def inflow(masks, up, mid, down):
    e0, e1, e2, w0, w1, w2, s0, s1 = masks
    zero = jnp.zeros_like(up)
    east = jnp.where(e0, up, zero) + jnp.where(e1, mid, zero) + jnp.where(e2, down, zero)
    west = jnp.where(w0, up, zero) + jnp.where(w1, mid, zero) + jnp.where(w2, down, zero)
    same = jnp.where(s0, up, zero) + jnp.where(s1, down, zero)
    return pltpu.roll(east, 1, 1) + pltpu.roll(west, W - 1, 1) + same


def outflow(h, liquid, orate, kind, lrate, ice, inv_por):
    q = orate * h * h / (h + 2.0)
    zero = jnp.zeros_like(q)
    moving = [jnp.where(kind == 0.0, q, zero)]
    for k in range(LAYERS):
        sat = jnp.minimum((liquid[k] + ice[k]) * inv_por, 1.0)
        moving.append((lrate * layer_speed[k]) * liquid[k] * (sat * sat))
    rest = [h - q] + [liquid[k] - moving[1 + k] for k in range(LAYERS)]
    return moving, rest, jnp.where(kind == 1.0, q, zero)


def settle(rest, arriving, ice_less_por):
    h = rest[0] + arriving[0]
    liquid = []
    for k in range(LAYERS):
        u = rest[1 + k] + arriving[1 + k]
        spill = jnp.maximum(u + ice_less_por[k], 0.0)
        h = h + (1000.0 * thickness[k]) * spill
        liquid.append(u - spill)
    return h, liquid


def kernel(
    nr,
    nc,
    rain_h,
    infil_h,
    por_h,
    liq_h,
    ice_h,
    dir_h,
    kind_h,
    orate_h,
    lrate_h,
    weight_h,
    out_liq,
    out_h,
    out_c,
    rain,
    infil,
    por,
    liq,
    ice,
    dir_v,
    kind_v,
    orate_v,
    lrate_v,
    weight_v,
    nat,
    stat,
    tstat,
    dirs,
    tdirs,
    coarse,
    tcoarse,
    moving,
    tmoving,
    rest,
    trest,
    zsend,
    zrecv,
    vsend,
    vrecv,
    csend,
    crecv,
    hsend,
    hrecv,
    bsend,
    brecv,
    in_sem,
    zs_sem,
    zh_sem,
    zr_sem,
    vs_sem,
    vr_sem,
    cs_sem,
    cr_sem,
    hs_sem,
    hr_sem,
    bs_sem,
    br_sem,
):
    mi = lax.axis_index("rows")
    mj = lax.axis_index("cols")
    has_up, has_down = mi > 0, mi < nr - 1
    has_left, has_right = mj > 0, mj < nc - 1

    copies = [
        pltpu.make_async_copy(src, dst, in_sem.at[n])
        for n, (src, dst) in enumerate(
            (
                (rain_h, rain),
                (infil_h, infil),
                (por_h, por),
                (liq_h, liq),
                (ice_h, ice),
                (weight_h, weight_v),
                (dir_h, dir_v),
                (kind_h, kind_v),
                (orate_h, orate_v),
                (lrate_h, lrate_v),
            )
        )
    ]
    for copy in copies:
        copy.start()

    barrier = pltpu.get_barrier_semaphore()

    def tell(i, j):
        pl.semaphore_signal(barrier, inc=1, device_id=(i, j), device_id_type=MESH)

    @pl.loop(1, nc)
    def _(d):
        tell(mi, lax.rem(mj + d, nc))

    sides = (
        (has_up, mi - 1, has_left, has_right, nc - 1),
        (has_down, mi + 1, has_left, has_right, 0),
    )
    for has, i, left, right, end in sides:

        @pl.when(has)
        def _(i=i, end=end):
            tell(i, mj)
            tell(i, end)

        @pl.when(has & left)
        def _(i=i):
            tell(i, mj - 1)

        @pl.when(has & right)
        def _(i=i):
            tell(i, mj + 1)

    for copy in copies[:5]:
        copy.wait()
    rain_x, por_x = rain[...], por[...]
    top_sat = (liq[0] + ice[0]) / por_x
    capacity = infil[...] * jnp.maximum(1.0 - top_sat, 0.1)
    excess = rain_x * rain_x / (rain_x + capacity)
    top = liq[0] + (rain_x - excess) / (1000.0 * thickness[0])
    strip = [excess, por_x, top] + [liq[k] for k in range(1, LAYERS)] + [ice[k] for k in range(LAYERS)]

    lane = iota((8, 128), 1)
    slot = tenth(lane * 10) * 0 + lax.shift_right_logical(lane * 2731, 16)
    t = lane - slot * 24
    for half in range(2):
        base = (iota((8, 128), 0) + 8 * half) * 16 - 1 + t
        inside = jnp.clip(base, 0, W - 1)
        index = inside & 127
        low = inside < 128
        for group in range(2):
            packed = jnp.zeros((8, 128), jnp.float32)
            for n in range(5):
                x = strip[group * 5 + n]
                a = jnp.broadcast_to(x[:, :128], (8, 128))
                b = jnp.broadcast_to(x[:, 128:], (8, 128))
                packed = jnp.where(slot == n, jnp.where(low, take(a, index), take(b, index)), packed)
            for s in range(8):
                zsend[8 * half + s, :, 128 * group : 128 * group + 128] = packed[s : s + 1]

    zrecv[mj] = zsend[mj]

    @pl.when(jnp.logical_not(has_down))
    def _():
        zrecv[CR] = zsend[mj]

    @pl.when(jnp.logical_not(has_up))
    def _():
        zrecv[CR + 1] = zsend[mj]

    incoming = nc - 1
    for has, i, left, right, end in sides:
        incoming += has.astype(jnp.int32) + (has & left).astype(jnp.int32) + (has & right).astype(jnp.int32)
    incoming += nc * ((has_up & (mj == 0)).astype(jnp.int32) + (has_down & (mj == nc - 1)).astype(jnp.int32))
    pl.semaphore_wait(barrier, incoming)

    def piece(k, i, s, sems):
        return pltpu.make_async_remote_copy(
            src_ref=zsend.at[k],
            dst_ref=zrecv.at[s],
            send_sem=sems.at[k],
            recv_sem=zr_sem.at[s],
            device_id=(i, k),
            device_id_type=MESH,
        )

    @pl.loop(1, nc)
    def _(d):
        piece(lax.rem(mj + d, nc), mi, mj, zs_sem).start()

    first_up = has_up & (mj == 0)
    last_down = has_down & (mj == nc - 1)

    @pl.when(first_up)
    def _():
        @pl.loop(0, nc)
        def _(k):
            piece(k, mi - 1, CR, zh_sem).start()

    @pl.when(last_down)
    def _():
        @pl.loop(0, nc)
        def _(k):
            piece(k, mi + 1, CR + 1, zh_sem).start()

    for copy in copies[5:]:
        copy.wait()
    lane160 = jnp.zeros((TILE, 96), jnp.float32)
    kind_x = kind_v[...].astype(jnp.float32)
    orate_x = jnp.where(kind_x == 2.0, 0.0, orate_v[...].astype(jnp.float32))
    natural = (
        dir_v[...].astype(jnp.float32),
        orate_x,
        kind_x,
        lrate_v[...].astype(jnp.float32),
        weight_v[...].astype(jnp.float32),
    )
    for f in range(FIELDS):
        nat[2 * f] = natural[f][:, :128]
        nat[2 * f + 1] = jnp.concatenate([natural[f][:, 128:], lane160], 1)

    def rows_of(f, rr):
        return jnp.concatenate(
            [nat.at[2 * f + half][pl.ds(rr, CR, stride=REFINE), :] for half in range(2)], 1
        )

    weights = [rows_of(SHARE, rr) for rr in range(REFINE)]
    total = functools.reduce(lambda a, b: a + b, weights)
    row_c, col_c = iota((W, W), 0), iota((W, W), 1)
    same_block = (tenth(row_c) == tenth(col_c)) & (row_c < TILE) & (col_c < TILE)
    mean_of = dot3(total, jnp.where(same_block, 1.0, 0.0).astype(jnp.bfloat16))
    wide = iota((CR, W), 1)
    per_mean = 100.0 / jnp.where(wide < TILE, mean_of, 1.0)
    for rr in range(REFINE):
        stat[SHARE, rr * CR : (rr + 1) * CR] = weights[rr] * per_mean
        for f in (ORATE, KIND, LRATE):
            stat[f, rr * CR : (rr + 1) * CR] = rows_of(f, rr)
        dirs[(rr + 1) * CR : (rr + 2) * CR] = rows_of(DIR, rr)

    def tile_rows(f, rr):
        if f == DIR:
            return dirs[(rr + 1) * CR : (rr + 2) * CR]
        return stat[f, rr * CR : (rr + 1) * CR]

    zero_row = jnp.zeros((1, W), jnp.float32)
    for f in range(FIELDS):
        off = CR if f == DIR else 0
        ref = dirs if f == DIR else stat.at[f]
        for p in range(HALO):
            vsend[0, HALO * f + p : HALO * f + p + 1] = ref[off + p * CR : off + p * CR + 1]
            r = off + (REFINE - HALO + p) * CR + CR - 1
            vsend[1, HALO * f + p : HALO * f + p + 1] = ref[r : r + 1]
    for v in range(2):
        vsend[v, 15:16] = zero_row
        csend[v, 0] = pltpu.roll(vsend[v, :, :128], 32, 1)
        csend[v, 1] = pltpu.roll(vsend[v, :, 128:], 96, 1)

    def vertical(v, i):
        return pltpu.make_async_remote_copy(
            src_ref=vsend.at[v],
            dst_ref=vrecv.at[v],
            send_sem=vs_sem.at[v],
            recv_sem=vr_sem.at[v],
            device_id=(i, mj),
            device_id_type=MESH,
        )

    def corner(v, s, i, j):
        return pltpu.make_async_remote_copy(
            src_ref=csend.at[v, s],
            dst_ref=crecv.at[v, s],
            send_sem=cs_sem.at[v, s],
            recv_sem=cr_sem.at[v, s],
            device_id=(i, j),
            device_id_type=MESH,
        )

    for v, (has, i, left, right, end) in enumerate(sides):

        @pl.when(has)
        def _(v=v, i=i):
            vertical(v, i).start()

        @pl.when(has & left)
        def _(v=v, i=i):
            corner(v, 0, i, mj - 1).start()

        @pl.when(has & right)
        def _(v=v, i=i):
            corner(v, 1, i, mj + 1).start()

    lane16 = iota((CR, 128), 1)
    for s in range(3):
        slab = jnp.zeros((CR, 128), jnp.float32)
        for u in range(4):
            rr = 4 * s + u
            if rr >= REFINE:
                break
            for f in range(FIELDS):
                x = tile_rows(f, rr)
                at = HALO * (FIELDS * u + f)
                a = pltpu.roll(x[:, :128], at, 1) if at else x[:, :128]
                b = pltpu.roll(x[:, 128:], (64 + at - 29) % 128, 1)
                slab = jnp.where((lane16 >= at) & (lane16 < at + HALO), a, slab)
                slab = jnp.where((lane16 >= 64 + at) & (lane16 < 64 + at + HALO), b, slab)
        hsend[s] = slab

    def sideways(n, j):
        return pltpu.make_async_remote_copy(
            src_ref=hsend,
            dst_ref=hrecv.at[n],
            send_sem=hs_sem.at[n],
            recv_sem=hr_sem.at[n],
            device_id=(mi, j),
            device_id_type=MESH,
        )

    @pl.when(has_left)
    def _():
        sideways(0, mj - 1).start()

    @pl.when(has_right)
    def _():
        sideways(1, mj + 1).start()

    for v, (has, i, left, right, end) in enumerate(sides):

        @pl.when(jnp.logical_not(has))
        def _(v=v):
            vrecv[1 - v] = jnp.zeros(vrecv.shape[1:], jnp.float32)

        @pl.when(jnp.logical_not(has & left))
        def _(v=v):
            crecv[1 - v, 1] = jnp.zeros((CR, 128), jnp.float32)

        @pl.when(jnp.logical_not(has & right))
        def _(v=v):
            crecv[1 - v, 0] = jnp.zeros((CR, 128), jnp.float32)

    @pl.when(jnp.logical_not(has_right))
    def _():
        hrecv[0] = jnp.zeros(hrecv.shape[1:], jnp.float32)

    @pl.when(jnp.logical_not(has_left))
    def _():
        hrecv[1] = jnp.zeros(hrecv.shape[1:], jnp.float32)

    @pl.loop(1, nc)
    def _(d):
        k = lax.rem(mj + d, nc)
        piece(k, mi, k, zs_sem).wait_recv()

    @pl.when(has_down)
    def _():
        piece(0, mi, CR, zh_sem).wait_recv()

    @pl.when(has_up)
    def _():
        piece(0, mi, CR + 1, zh_sem).wait_recv()

    sub8 = iota((8, W), 0)
    under = jnp.broadcast_to(zrecv[CR], (8, W))
    over = jnp.broadcast_to(zrecv[CR + 1], (8, W))
    rows = [jnp.concatenate([zrecv[8 * n + s] for s in range(8)], 0) for n in range(2)]
    rows = jnp.concatenate(rows + [jnp.where(sub8 < 4, under, over)], 0)
    wide24 = iota((24, 128), 1)
    column = (
        1 + tenth(wide24),
        jnp.where(wide24 >= 125, 0, jnp.minimum(1 + tenth(wide24 + 128), 17)),
    )
    wide_fields = []
    for f in range(COARSE):
        g = rows[:, 128 * (f // 5) : 128 * (f // 5) + 128]
        at = 24 * (f % 5)
        wide_fields.append(jnp.concatenate([take(g, column[0] + at), take(g, column[1] + at)], 1))
    excess_w, por_w = wide_fields[0], wide_fields[1]
    ice_w = wide_fields[2 + LAYERS :]
    kept = [1.0 / por_w] + ice_w + [x - por_w for x in ice_w]
    for n, x in enumerate(kept):
        coarse[n] = x[:CR]
        tcoarse[n] = x[CR:]

    for v, (has, i, left, right, end) in enumerate(sides):

        @pl.when(has)
        def _(v=v):
            vertical(1 - v, mi).wait_recv()

        @pl.when(has & left)
        def _(v=v):
            corner(1 - v, 1, mi, mj).wait_recv()

        @pl.when(has & right)
        def _(v=v):
            corner(1 - v, 0, mi, mj).wait_recv()

    @pl.when(has_right)
    def _():
        sideways(0, mj).wait_recv()

    @pl.when(has_left)
    def _():
        sideways(1, mj).wait_recv()

    right_halo = (lane16 >= 32) & (lane16 < 32 + HALO)
    left_halo = lane16 >= 128 - HALO

    for v in range(2):
        far = jnp.where(right_halo, crecv[v, 0], jnp.where(left_halo, crecv[v, 1], 0.0))
        far = jnp.where(lane16 < 32, vrecv[v, :, 128:], far)
        vrecv[v, :, 128:] = far
    zero3 = jnp.zeros((2, W), jnp.float32)
    for f in range(FIELDS):
        x = jnp.concatenate(
            [vrecv[0, HALO * f : HALO * f + HALO], zero3, vrecv[1, HALO * f : HALO * f + HALO]], 0
        )
        tstat[f] = x

    for s in range(3):
        slab = jnp.where(lane16 < 64, hrecv[0, s], hrecv[1, s])
        for u in range(4):
            rr = 4 * s + u
            if rr >= REFINE:
                break
            for f in range(FIELDS):
                at = HALO * (FIELDS * u + f)
                from_right = pltpu.roll(slab, (32 - at) % 128, 1)
                from_left = pltpu.roll(slab, (125 - 64 - at) % 128, 1)
                ref = dirs if f == DIR else stat.at[f]
                r = rr * CR + (CR if f == DIR else 0)
                x = ref[r : r + CR, 128:]
                x = jnp.where(right_halo, from_right, jnp.where(left_halo, from_left, x))
                ref[r : r + CR, 128:] = x

    def wrap(first, last, tail):
        up = pltpu.roll(jnp.concatenate([last, tail], 0), 1, 0)
        down = pltpu.roll(jnp.concatenate([first, tail], 0), CR + 7, 0)
        return up, down

    up, down = wrap(dirs[CR : 2 * CR], dirs[TILE : TILE + CR], tstat[DIR])
    dirs[:CR], tdirs[0] = up[:CR], up[CR:]
    dirs[TILE + CR :], tdirs[1] = down[:CR], down[CR:]

    def finish_wrap(b):
        for f in range(FIELDS):
            up, down = wrap(moving[b, f, CR : 2 * CR], moving[b, f, TILE : TILE + CR], tmoving[b, f])
            moving[b, f, :CR], tmoving[2 + b, f] = up[:CR], up[CR:]
            moving[b, f, TILE + CR :], tmoving[4 + b, f] = down[:CR], down[CR:]

    def main_in(b, r):
        d = [dirs[pl.ds(r + n * CR, CR), :] for n in range(3)]
        masks = inflow_masks(*d)
        arriving = [
            inflow(masks, *[moving[b, f, pl.ds(r + n * CR, CR), :] for n in range(3)])
            for f in range(FIELDS)
        ]
        left = [rest[f, pl.ds(r, CR), :] for f in range(FIELDS)]
        return settle(left, arriving, [coarse[1 + LAYERS + k] for k in range(LAYERS)])

    def main_out(b, r, h, liquid):
        move, left, chan = outflow(
            h,
            liquid,
            stat[ORATE, pl.ds(r, CR), :],
            stat[KIND, pl.ds(r, CR), :],
            stat[LRATE, pl.ds(r, CR), :],
            [coarse[1 + k] for k in range(LAYERS)],
            coarse[0],
        )
        for f in range(FIELDS):
            moving[b, f, pl.ds(r + CR, CR), :] = move[f]
            rest[f, pl.ds(r, CR), :] = left[f]
        return chan

    def tail_in(b):
        masks = inflow_masks(tdirs[0], tstat[DIR], tdirs[1])
        arriving = [
            inflow(masks, tmoving[2 + b, f], tmoving[b, f], tmoving[4 + b, f]) for f in range(FIELDS)
        ]
        return settle(
            [trest[f] for f in range(FIELDS)], arriving, [tcoarse[1 + LAYERS + k] for k in range(LAYERS)]
        )

    def tail_out(b, h, liquid):
        move, left, _ = outflow(
            h,
            liquid,
            tstat[ORATE],
            tstat[KIND],
            tstat[LRATE],
            [tcoarse[1 + k] for k in range(LAYERS)],
            tcoarse[0],
        )
        for f in range(FIELDS):
            tmoving[b, f] = move[f]
            trest[f] = left[f]

    def row_at(rr):
        return pl.multiple_of(rr * CR, CR)

    zero16 = jnp.zeros((CR, W), jnp.float32)
    excess_m = excess_w[:CR]
    liquid_m = [x[:CR] for x in wide_fields[2 : 2 + LAYERS]]

    def first(rr, chan):
        r = row_at(rr)
        return chan + main_out(0, r, excess_m * stat[SHARE, pl.ds(r, CR), :], liquid_m)

    chan = lax.fori_loop(0, REFINE, first, zero16)
    tail_out(0, excess_w[CR:] * tstat[SHARE], [x[CR:] for x in wide_fields[2 : 2 + LAYERS]])
    finish_wrap(0)

    for b in range(2):

        def middle(rr, chan, b=b):
            r = row_at(rr)
            return chan + main_out(1 - b, r, *main_in(b, r))

        chan = lax.fori_loop(0, REFINE, middle, chan)
        tail_out(1 - b, *tail_in(b))
        finish_wrap(1 - b)

    def last(rr, sums):
        h, liquid = main_in(0, row_at(rr))
        return tuple(a + x for a, x in zip(sums, liquid + [h]))

    sums = lax.fori_loop(0, REFINE, last, (zero16,) * (LAYERS + 1))

    row_p, col_p = iota((W, 128), 0), iota((W, 128), 1)
    to_block = (tenth(row_p) == col_p) & (row_p < TILE)
    means = dot3(jnp.concatenate(sums + (chan,), 0), jnp.where(to_block, 1.0, 0.0).astype(jnp.bfloat16)) * 0.01
    back = means[:CR]
    for n in range(1, LAYERS + 2):
        back = back + pltpu.roll(means[n * CR : (n + 1) * CR], 16 * n, 1)
    for s in range(CR):
        bsend[s] = back[s : s + 1]
    brecv[mj] = bsend[mj]

    def answer(k, s):
        return pltpu.make_async_remote_copy(
            src_ref=bsend.at[k],
            dst_ref=brecv.at[s],
            send_sem=bs_sem.at[k],
            recv_sem=br_sem.at[s],
            device_id=(mi, k),
            device_id_type=MESH,
        )

    @pl.loop(1, nc)
    def _(d):
        answer(lax.rem(mj + d, nc), mj).start()

    @pl.loop(1, nc)
    def _(d):
        piece(lax.rem(mj + d, nc), mi, mj, zs_sem).wait_send()

    @pl.when(first_up | last_down)
    def _():
        @pl.loop(0, nc)
        def _(k):
            piece(k, mi, CR, zh_sem).wait_send()

    for v, (has, i, left, right, end) in enumerate(sides):

        @pl.when(has)
        def _(v=v, i=i):
            vertical(v, i).wait_send()

        @pl.when(has & left)
        def _(v=v, i=i):
            corner(v, 0, i, mj - 1).wait_send()

        @pl.when(has & right)
        def _(v=v, i=i):
            corner(v, 1, i, mj + 1).wait_send()

    @pl.when(has_left)
    def _():
        sideways(0, mj - 1).wait_send()

    @pl.when(has_right)
    def _():
        sideways(1, mj + 1).wait_send()

    @pl.loop(1, nc)
    def _(d):
        k = lax.rem(mj + d, nc)
        answer(k, k).wait_recv()

    gather = iota((8, 128), 0) * 16 + (lane & 15)
    gather = jnp.minimum(gather, 127)
    owner = lax.shift_right_logical(lane, 4)
    for half in range(2):
        out = jnp.zeros((8, 128), jnp.float32)
        for s in range(8):
            x = jnp.broadcast_to(brecv[8 * half + s], (8, 128))
            out = jnp.where(owner == s, take(x, gather), out)
        lanes = slice(128 * half, 128 * half + 128)
        for k in range(LAYERS):
            out_liq[k, :, lanes] = out[k : k + 1]
        out_h[:, lanes] = out[LAYERS : LAYERS + 1]
        out_c[:, lanes] = out[LAYERS + 1 : LAYERS + 2]

    @pl.loop(1, nc)
    def _(d):
        k = lax.rem(mj + d, nc)
        answer(k, k).wait_send()


def solution(mesh):
    nr, nc = mesh.shape["rows"], mesh.shape["cols"]
    f32, bf16 = jnp.float32, jnp.bfloat16

    def step(*args):
        v = pltpu.VMEM
        dma = pltpu.SemaphoreType.DMA
        return pl.pallas_call(
            functools.partial(kernel, nr, nc),
            out_shape=(
                jax.ShapeDtypeStruct((LAYERS, 1, W), f32),
                jax.ShapeDtypeStruct((1, W), f32),
                jax.ShapeDtypeStruct((1, W), f32),
            ),
            in_specs=[pl.BlockSpec(memory_space=pl.ANY)] * 10,
            out_specs=[pl.BlockSpec(memory_space=pltpu.VMEM)] * 3,
            scratch_shapes=[
                v((1, W), f32),
                v((1, W), f32),
                v((1, W), f32),
                v((LAYERS, 1, W), f32),
                v((LAYERS, 1, W), f32),
                v((TILE, TILE), jnp.int32),
                v((TILE, TILE), jnp.int32),
                v((TILE, TILE), bf16),
                v((TILE, TILE), bf16),
                v((TILE, TILE), bf16),
                v((2 * FIELDS, TILE, 128), f32),
                v((FIELDS, TILE, W), f32),
                v((FIELDS, 8, W), f32),
                v((TILE + 2 * CR, W), f32),
                v((2, 8, W), f32),
                v((1 + 2 * LAYERS, CR, W), f32),
                v((1 + 2 * LAYERS, 8, W), f32),
                v((2, FIELDS, TILE + 2 * CR, W), f32),
                v((6, FIELDS, 8, W), f32),
                v((FIELDS, TILE, W), f32),
                v((FIELDS, 8, W), f32),
                v((CR, 1, W), f32),
                v((CR + 2, 1, W), f32),
                v((2, CR, W), f32),
                v((2, CR, W), f32),
                v((2, 2, CR, 128), f32),
                v((2, 2, CR, 128), f32),
                v((3, CR, 128), f32),
                v((2, 3, CR, 128), f32),
                v((CR, 1, 128), f32),
                v((CR, 1, 128), f32),
                dma((10,)),
                dma((CR,)),
                dma((CR,)),
                dma((CR + 2,)),
                dma((2,)),
                dma((2,)),
                dma((2, 2)),
                dma((2, 2)),
                dma((2,)),
                dma((2,)),
                dma((CR,)),
                dma((CR,)),
            ],
            compiler_params=pltpu.CompilerParams(
                collective_id=0, has_side_effects=True, vmem_limit_bytes=32 * 1024 * 1024
            ),
        )(*args)

    return jax.shard_map(
        step,
        mesh=mesh,
        in_specs=(
            P(("rows", "cols"), None),
            P(("rows", "cols"), None),
            P(("rows", "cols"), None),
            P(None, ("rows", "cols"), None),
            P(None, ("rows", "cols"), None),
            P("rows", "cols"),
            P("rows", "cols"),
            P("rows", "cols"),
            P("rows", "cols"),
            P("rows", "cols"),
        ),
        out_specs=(
            P(None, ("rows", "cols"), None),
            P(("rows", "cols"), None),
            P(("rows", "cols"), None),
        ),
        check_vma=False,
    )
```

time: 186 us -> 35.2 us (0.19); the launches traced: 182 us -> 34.8 us
  starting transfers between devices: 60.2 us -> 0 us
  blocking collectives: 52.8 us -> 0 us
  local copies, waits for them, and re-layouts: 36.2 us -> 9.61 us
  Pallas kernels: 0 us -> 24.5 us
  waiting for transfers between devices: 16.5 us -> 0 us
  other arithmetic: 14.8 us -> 0 us
    ppermute x16 -> x0, starting transfers between devices: 60.2 us -> none  [the longest x8 35.7 us: extended(): lax.ppermute(tail, axis, [(i, (i + 1) % count) for i in range(ends)])]
    all_gather x2 -> x0, blocking collectives: 52.8 us -> none  [the longest x1 32.7 us: body(): cols_all = lax.all_gather(stack_back, 'cols', axis=2, tiled=True)]
    pallas_call x0 -> x1, Pallas kernels: none -> 24.5 us  [step(): pl.pallas_call(functools.partial(kernel, nr, nc), out_shape=(jax.ShapeDty...]
    reshape x9 -> x0, local copies, waits for them, and re-layouts: 17.6 us -> none  [the longest x5 10.8 us: expand_coarse(): return grown.reshape(lead + (nrow * REFINE, ncol * REFINE))]
    ppermute x16 -> x0, waiting for transfers between devices: 16.5 us -> none  [the longest x8 16.5 us: extended(): lax.ppermute(tail, axis, [(i, (i + 1) % count) for i in range(ends)])]
    slice x20 -> x0, local copies, waits for them, and re-layouts: 8.5 us -> none  [the longest x2 4.77 us: body(): return (back[:LAYERS], back[LAYERS], back[LAYERS + 1])]
    unnamed x73 -> x23, local copies, waits for them, and re-layouts: 3.27 us -> 9.61 us
    broadcast_in_dim x5 -> x0, local copies, waits for them, and re-layouts: 5.94 us -> none  [expand_coarse(): jnp.broadcast_to(coarse[..., :, None, :, None], lead + (nrow, REFINE, nco...]
  transfers between devices with their start and end apart: 16 -> 0, of which waited for: 6 -> 0; matrix products, arithmetic and copies ran while one was open for 12% -> 0% of each run, Pallas kernels for 0% -> 0%
where the time goes in v1:
time: 35.2 us; the launch traced here: 34.8 us
  Pallas kernels  24.5 us (70%)
  local copies, waits for them, and re-layouts  9.61 us (27%)
  between operations  0.66 us (2%)
    pallas_call x1, Pallas kernels, step(): pl.pallas_call(functools.partial(kernel, nr, nc), out_shape=(jax.ShapeDty...  24.5 us
    unnamed x23, local copies, waits for them, and re-layouts  9.61 us

profile of v1, /device:TPU:6, one launch (start us, length us, event | category | flops | bytes accessed | tf_op | source)
XLA Modules:
  0.0 34.8 jit_solution(3584327953681787450)
XLA Ops:
  0.6 0.0 copy-start
  0.6 0.9 %copy-done = s32[160,160]{1,0:T(8,128)S(1)} copy-done((s32[160,160]{1,0:T(8,128)S(1)}, s32[160,160]{1,0:T(8,128)}, u32[]{:S(2)}) %copy-start) | copy-done | bytes 102424
  1.6 0.0 copy-start.1
  1.6 0.9 %copy-done.1 = s32[160,160]{1,0:T(8,128)S(1)} copy-done((s32[160,160]{1,0:T(8,128)S(1)}, s32[160,160]{1,0:T(8,128)}, u32[]{:S(2)}) %copy-start.1) | copy-done | bytes 102424
  2.5 0.0 copy-start.2
  2.5 0.9 %copy-done.2 = bf16[160,160]{1,0:T(8,128)(2,1)S(1)} copy-done((bf16[160,160]{1,0:T(8,128)(2,1)S(1)}, bf16[160,160]{1,0:T(8,128)(2,1)}, u32[]{:S(2)}) %copy-start.2) | copy-done | bytes 51224
  3.4 0.0 copy-start.3
  3.4 0.9 %copy-done.3 = bf16[160,160]{1,0:T(8,128)(2,1)S(1)} copy-done((bf16[160,160]{1,0:T(8,128)(2,1)S(1)}, bf16[160,160]{1,0:T(8,128)(2,1)}, u32[]{:S(2)}) %copy-start.3) | copy-done | bytes 51224
  4.2 0.0 copy-start.4
  4.2 0.9 %copy-done.4 = bf16[160,160]{1,0:T(8,128)(2,1)S(1)} copy-done((bf16[160,160]{1,0:T(8,128)(2,1)S(1)}, bf16[160,160]{1,0:T(8,128)(2,1)}, u32[]{:S(2)}) %copy-start.4) | copy-done | bytes 51224
  5.1 0.0 copy-start.5
  5.1 0.7 %copy-done.5 = f32[4,1,256]{2,1,0:T(1,128)S(1)} copy-done((f32[4,1,256]{2,1,0:T(1,128)S(1)}, f32[4,1,256]{2,1,0:T(1,128)}, u32[]{:S(2)}) %copy-start.5) | copy-done | bytes 4120
  5.8 0.0 copy-start.6
  5.8 0.7 %copy-done.6 = f32[4,1,256]{2,1,0:T(1,128)S(1)} copy-done((f32[4,1,256]{2,1,0:T(1,128)S(1)}, f32[4,1,256]{2,1,0:T(1,128)}, u32[]{:S(2)}) %copy-start.6) | copy-done | bytes 4120
  6.5 0.0 copy-start.7
  6.5 0.7 %copy-done.7 = f32[1,256]{1,0:T(1,128)S(1)} copy-done((f32[1,256]{1,0:T(1,128)S(1)}, f32[1,256]{1,0:T(1,128)}, u32[]{:S(2)}) %copy-start.7) | copy-done | bytes 1048
  7.2 0.0 copy-start.8
  7.2 0.7 %copy-done.8 = f32[1,256]{1,0:T(1,128)S(1)} copy-done((f32[1,256]{1,0:T(1,128)S(1)}, f32[1,256]{1,0:T(1,128)}, u32[]{:S(2)}) %copy-start.8) | copy-done | bytes 1048
  7.9 0.0 copy-start.9
  7.9 0.7 %copy-done.9 = f32[1,256]{1,0:T(1,128)S(1)} copy-done((f32[1,256]{1,0:T(1,128)S(1)}, f32[1,256]{1,0:T(1,128)}, u32[]{:S(2)}) %copy-start.9) | copy-done | bytes 1048
  8.5 24.5 %shard_map.121 = (f32[4,1,256]{2,1,0:T(1,128)S(1)}, f32[1,256]{1,0:T(1,128)S(1)}, f32[1,256]{1,0:T(1,128)S(1)}) custom-call(f32[1,256]{1,0:T(1,128)S(1)} %copy-done.7, f32[1,256]{1,0:T(1,128)S(1)} %copy-done.8, f32[1,256]{1,0:T(1,128)S(1)} %copy-done.9, f32[4,1,256]{2,1,0:T(1,128)S(1)} %copy-done.5, f32[4,1,256]{2,1,0:T(1,128)S(1)} %copy-done.6, ...), custom_call_target="tpu_custom_call" | custom-call | tf_op jit(solution)/shard_map/pallas_call | solution.py:692
  33.1 0.6 %copy.16 = f32[4,1,256]{2,1,0:T(1,128)} copy(f32[4,1,256]{2,1,0:T(1,128)S(1)} %get-tuple-element.6) | data formatting | bytes 8192
  33.7 0.6 %copy.17 = f32[1,256]{1,0:T(1,128)} copy(f32[1,256]{1,0:T(1,128)S(1)} %get-tuple-element.7) | data formatting | bytes 2048
  34.2 0.6 %copy.18 = f32[1,256]{1,0:T(1,128)} copy(f32[1,256]{1,0:T(1,128)S(1)} %get-tuple-element.8) | data formatting | bytes 2048
Async XLA Ops:
  0.6 0.9 %copy-start = (s32[160,160]{1,0:T(8,128)S(1)}, s32[160,160]{1,0:T(8,128)}, u32[]{:S(2)}) copy-start(s32[160,160]{1,0:T(8,128)} %dir_h.1) | copy-start | bytes 307204
  1.6 0.9 %copy-start.1 = (s32[160,160]{1,0:T(8,128)S(1)}, s32[160,160]{1,0:T(8,128)}, u32[]{:S(2)}) copy-start(s32[160,160]{1,0:T(8,128)} %kind_h.1) | copy-start | bytes 307204
  2.5 0.9 %copy-start.2 = (bf16[160,160]{1,0:T(8,128)(2,1)S(1)}, bf16[160,160]{1,0:T(8,128)(2,1)}, u32[]{:S(2)}) copy-start(bf16[160,160]{1,0:T(8,128)(2,1)} %orate_h.1) | copy-start | bytes 153604
  3.4 0.9 %copy-start.3 = (bf16[160,160]{1,0:T(8,128)(2,1)S(1)}, bf16[160,160]{1,0:T(8,128)(2,1)}, u32[]{:S(2)}) copy-start(bf16[160,160]{1,0:T(8,128)(2,1)} %lrate_h.1) | copy-start | bytes 153604
  4.2 0.9 %copy-start.4 = (bf16[160,160]{1,0:T(8,128)(2,1)S(1)}, bf16[160,160]{1,0:T(8,128)(2,1)}, u32[]{:S(2)}) copy-start(bf16[160,160]{1,0:T(8,128)(2,1)} %weight_h.1) | copy-start | bytes 153604
  5.1 0.7 %copy-start.5 = (f32[4,1,256]{2,1,0:T(1,128)S(1)}, f32[4,1,256]{2,1,0:T(1,128)}, u32[]{:S(2)}) copy-start(f32[4,1,256]{2,1,0:T(1,128)} %liq_h.1) | copy-start | bytes 12292
  5.8 0.7 %copy-start.6 = (f32[4,1,256]{2,1,0:T(1,128)S(1)}, f32[4,1,256]{2,1,0:T(1,128)}, u32[]{:S(2)}) copy-start(f32[4,1,256]{2,1,0:T(1,128)} %ice_h.1) | copy-start | bytes 12292
  6.5 0.7 %copy-start.7 = (f32[1,256]{1,0:T(1,128)S(1)}, f32[1,256]{1,0:T(1,128)}, u32[]{:S(2)}) copy-start(f32[1,256]{1,0:T(1,128)} %rain_h.1) | copy-start | bytes 3076
  7.2 0.7 %copy-start.8 = (f32[1,256]{1,0:T(1,128)S(1)}, f32[1,256]{1,0:T(1,128)}, u32[]{:S(2)}) copy-start(f32[1,256]{1,0:T(1,128)} %infil_h.1) | copy-start | bytes 3076
  7.9 0.7 %copy-start.9 = (f32[1,256]{1,0:T(1,128)S(1)}, f32[1,256]{1,0:T(1,128)}, u32[]{:S(2)}) copy-start(f32[1,256]{1,0:T(1,128)} %por_h.1) | copy-start | bytes 3076

commit v2 on v1

v2 whole, which is shorter than its diff:
```python
import functools
import math

import jax
import jax.numpy as jnp
from jax import lax
from jax.experimental import pallas as pl
from jax.experimental.pallas import tpu as pltpu
from jax.sharding import PartitionSpec as P

MESH = pl.DeviceIdType.MESH
REFINE = 10
LAYERS = 4
TILE = 160
CR = 16
W = 256
HALO = 3
ROWS = 2 * CR

thickness = (0.1, 0.3, 0.6, 1.0)
layer_speed = (1.0, 0.8, 0.6, 0.4)

DIR, ORATE, KIND, LRATE, SHARE = range(5)
FIELDS = 5
COARSE = 10


FAR_FIRST = sorted(
    ((z, y, c) for z in range(2) for y in range(4) for c in range(2) if z + y + c),
    key=lambda p: -(p[0] + min(p[1], 4 - p[1])),
)


def others(j):
    z, y, c = j // 8, (j // 2) % 4, j % 2
    return [((z + dz) % 2) * 8 + ((y + dy) % 4) * 2 + (c + dc) % 2 for dz, dy, dc in FAR_FIRST]


def iota(shape, dim):
    return lax.broadcasted_iota(jnp.int32, shape, dim)


def take(x, index):
    return jnp.take_along_axis(x, index, axis=1, mode="promise_in_bounds")


def tenth(x):
    return lax.shift_right_logical(x * 6554, 16)


def split3(x):
    hi = x.astype(jnp.bfloat16)
    r = x - hi.astype(jnp.float32)
    mid = r.astype(jnp.bfloat16)
    lo = (r - mid.astype(jnp.float32)).astype(jnp.bfloat16)
    return jnp.concatenate([hi, mid, lo], 0)


def split2(x):
    hi = x.astype(jnp.bfloat16)
    lo = (x - hi.astype(jnp.float32)).astype(jnp.bfloat16)
    return jnp.concatenate([hi, lo], 0)


def dot3(x, ones):
    n = x.shape[0]
    y = jnp.dot(split3(x), ones, preferred_element_type=jnp.float32)
    return y[:n] + y[n : 2 * n] + y[2 * n :]


def dot2(x, ones):
    n = x.shape[0]
    y = jnp.dot(split2(x), ones, preferred_element_type=jnp.float32)
    return y[:n] + y[n:]


def inflow_masks(d_up, d_mid, d_down):
    return (
        d_up == 1.0,
        d_mid == 0.0,
        d_down == 7.0,
        d_up == 3.0,
        d_mid == 4.0,
        d_down == 5.0,
        d_up == 2.0,
        d_down == 6.0,
    )


def inflow(masks, up, mid, down):
    e0, e1, e2, w0, w1, w2, s0, s1 = masks
    zero = jnp.zeros_like(up)
    east = jnp.where(e0, up, zero) + jnp.where(e1, mid, zero) + jnp.where(e2, down, zero)
    west = jnp.where(w0, up, zero) + jnp.where(w1, mid, zero) + jnp.where(w2, down, zero)
    same = jnp.where(s0, up, zero) + jnp.where(s1, down, zero)
    return same + pltpu.roll(east, 1, 1) + pltpu.roll(west, 127, 1)


def outflow(h, liquid, orate, kind, lrate, ice, per_pore):
    q = orate * h * (h / (h + 2.0))
    zero = jnp.zeros_like(q)
    moving = [jnp.where(kind == 0.0, q, zero)]
    rest = [h - q]
    for k in range(LAYERS):
        sat = jnp.minimum((liquid[k] + ice[k]) * per_pore[k], math.sqrt(layer_speed[k]))
        lateral = (lrate * liquid[k]) * (sat * sat)
        moving.append(lateral)
        rest.append(liquid[k] - lateral)
    return moving, rest, jnp.where(kind == 1.0, q, zero)


def settle(rest, arriving, room):
    h = rest[0] + arriving[0]
    liquid = []
    for k in range(LAYERS):
        u = rest[1 + k] + arriving[1 + k]
        h = h + jnp.maximum(u - room[k], 0.0)
        liquid.append(jnp.minimum(u, room[k]))
    return h, liquid


def kernel(
    nr,
    nc,
    rain_h,
    infil_h,
    por_h,
    liq_h,
    ice_h,
    dir_h,
    kind_h,
    orate_h,
    lrate_h,
    weight_h,
    out_liq,
    out_h,
    out_c,
    rain,
    infil,
    por,
    liq,
    ice,
    dir_v,
    kind_v,
    orate_v,
    lrate_v,
    weight_v,
    nat,
    stat,
    dirs,
    coarse,
    moving,
    rest,
    sstat,
    scoarse,
    zsend,
    zrecv,
    vsend,
    vrecv,
    csend,
    crecv,
    hsend,
    hrecv,
    bsend,
    brecv,
    in_sem,
    zs_sem,
    zh_sem,
    zr_sem,
    vs_sem,
    vr_sem,
    cs_sem,
    cr_sem,
    hs_sem,
    hr_sem,
    bs_sem,
    br_sem,
    row_sem,
    relay_sem,
):
    mi = lax.axis_index("rows")
    mj = lax.axis_index("cols")
    has_up, has_down = mi > 0, mi < nr - 1
    has_left, has_right = mj > 0, mj < nc - 1

    copies = [
        pltpu.make_async_copy(src, dst, in_sem.at[n])
        for n, (src, dst) in enumerate(
            (
                (rain_h, rain),
                (infil_h, infil),
                (por_h, por),
                (liq_h, liq),
                (ice_h, ice),
                (weight_h, weight_v),
                (dir_h, dir_v),
                (kind_h, kind_v),
                (orate_h, orate_v),
                (lrate_h, lrate_v),
            )
        )
    ]
    for copy in copies:
        copy.start()

    barrier = pltpu.get_barrier_semaphore()
    lead = nc - 2
    is_lead = mj == lead

    def tell(i, j):
        pl.semaphore_signal(barrier, inc=1, device_id=(i, j), device_id_type=MESH)

    @pl.when(jnp.logical_not(is_lead))
    def _():
        tell(mi, lead)

    sides = (
        (has_up, mi - 1, has_left, has_right, nc - 1),
        (has_down, mi + 1, has_left, has_right, 0),
    )
    for has, i, left, right, end in sides:

        @pl.when(has)
        def _(i=i, end=end):
            tell(i, end)

        @pl.when(has & jnp.logical_not(is_lead))
        def _(i=i):
            tell(i, mj)

        @pl.when(has & left & (mj - 1 != lead))
        def _(i=i):
            tell(i, mj - 1)

        @pl.when(has & right & (mj + 1 != lead))
        def _(i=i):
            tell(i, mj + 1)

    for copy in copies[:5]:
        copy.wait()
    rain_x, por_x = rain[...], por[...]
    top_sat = (liq[0] + ice[0]) / por_x
    capacity = infil[...] * jnp.maximum(1.0 - top_sat, 0.1)
    excess = rain_x * rain_x / (rain_x + capacity)
    top = liq[0] + (rain_x - excess) / (1000.0 * thickness[0])
    strip = [excess, por_x, top] + [liq[k] for k in range(1, LAYERS)] + [ice[k] for k in range(LAYERS)]

    lane = iota((8, 128), 1)
    slot = tenth(lane * 10) * 0 + lax.shift_right_logical(lane * 2731, 16)
    t = lane - slot * 24
    for half in range(2):
        base = (iota((8, 128), 0) + 8 * half) * 16 - 1 + t
        inside = jnp.clip(base, 0, W - 1)
        index = inside & 127
        low = inside < 128
        for group in range(2):
            packed = jnp.zeros((8, 128), jnp.float32)
            for n in range(5):
                x = strip[group * 5 + n]
                a = jnp.broadcast_to(x[:, :128], (8, 128))
                b = jnp.broadcast_to(x[:, 128:], (8, 128))
                packed = jnp.where(slot == n, jnp.where(low, take(a, index), take(b, index)), packed)
            for s in range(8):
                zsend[8 * half + s, :, 128 * group : 128 * group + 128] = packed[s : s + 1]

    zrecv[mj] = zsend[mj]

    @pl.when(jnp.logical_not(has_down))
    def _():
        zrecv[CR] = zsend[mj]

    @pl.when(jnp.logical_not(has_up))
    def _():
        zrecv[CR + 1] = zsend[mj]

    @pl.when(is_lead)
    def _():
        pl.semaphore_wait(barrier, nc - 1)
        for k in range(nc):
            if k != lead:
                pl.semaphore_signal(row_sem, inc=1, device_id=(mi, k), device_id_type=MESH)

    @pl.when(jnp.logical_not(is_lead))
    def _():
        pl.semaphore_wait(row_sem, 1)

    def piece(k, i, s, send, arrive):
        return pltpu.make_async_remote_copy(
            src_ref=zsend.at[k],
            dst_ref=zrecv.at[s],
            send_sem=send,
            recv_sem=arrive,
            device_id=(i, k),
            device_id_type=MESH,
        )

    def row_pieces():
        return pltpu.make_async_remote_copy(
            src_ref=zsend.at[: nc - 1],
            dst_ref=zrecv.at[: nc - 1],
            send_sem=zs_sem,
            recv_sem=zr_sem.at[0],
            device_id=(mi, mj),
            device_id_type=MESH,
        )

    for k in others(mj):
        piece(k, mi, mj, zs_sem, zr_sem.at[0]).start()

    first_up = has_up & (mj == 0)
    last_down = has_down & (mj == nc - 1)

    for copy in copies[5:]:
        copy.wait()
    kind_x = kind_v[...].astype(jnp.float32)
    natural = (
        dir_v[...].astype(jnp.float32),
        jnp.where(kind_x == 2.0, 0.0, orate_v[...].astype(jnp.float32)),
        kind_x,
        lrate_v[...].astype(jnp.float32),
        weight_v[...].astype(jnp.float32),
    )
    no_lanes = jnp.zeros((TILE, 96), jnp.float32)
    for f in range(FIELDS):
        nat[2 * f] = natural[f][:, :128]
        nat[2 * f + 1] = jnp.concatenate([natural[f][:, 128:], no_lanes], 1)

    lane16 = iota((CR, 128), 1)

    def halves(a, b):
        right = jnp.where(lane16 < 51, pltpu.roll(a, 51, 1), pltpu.roll(b, 51, 1))
        return jnp.concatenate([pltpu.roll(a, HALO, 1), right], 0)

    def rows_of(f, rr):
        return [nat.at[2 * f + half][pl.ds(rr, CR, stride=REFINE), :] for half in range(2)]

    def field(f):
        return (dirs, ROWS) if f == DIR else (stat.at[f], 0)

    def put(f, rr, x):
        ref, off = field(f)
        ref[off + rr * ROWS : off + (rr + 1) * ROWS] = x

    def get(f, rr):
        ref, off = field(f)
        return ref[off + rr * ROWS : off + (rr + 1) * ROWS]

    weights = [rows_of(SHARE, rr) for rr in range(REFINE)]
    total = [functools.reduce(lambda a, b: a + b, [w[half] for w in weights]) for half in range(2)]
    row_c, col_c = iota((W, W), 0), iota((W, W), 1)
    same_block = (tenth(row_c) == tenth(col_c)) & (row_c < TILE) & (col_c < TILE)
    sums = dot3(jnp.concatenate(total, 1), jnp.where(same_block, 1.0, 0.0).astype(jnp.bfloat16))
    per_mean = 100.0 / jnp.where(iota((CR, W), 1) < TILE, sums, 1.0)
    shares = [[w[half] * per_mean[:, 128 * half : 128 * half + 128] for half in range(2)] for w in weights]

    for v in range(2):
        r = v * (TILE - HALO)
        for half in range(2):
            for f in range(SHARE):
                vsend[v, half, HALO * f : HALO * f + HALO] = nat[2 * f + half, r : r + HALO]
            for p in range(HALO):
                x = shares[p + v * (REFINE - HALO)][half][v * (CR - 1) : v * (CR - 1) + 1]
                vsend[v, half, HALO * SHARE + p : HALO * SHARE + p + 1] = x
            vsend[v, half, HALO * FIELDS :] = jnp.zeros((1, 128), jnp.float32)
        x = halves(vsend[v, 0], vsend[v, 1])
        vsend[v, 0], vsend[v, 1] = x[:CR], x[CR:]
        for half, at in ((0, HALO), (1, 80)):
            place = lane16 - HALO * iota((CR, 128), 0)
            end = take(x[half * CR : half * CR + CR], jnp.clip(place + at, 0, 127))
            end = jnp.where((place >= 0) & (place < HALO), end, 0.0)
            csend[v, half] = jnp.sum(end, 0, keepdims=True)

    def slab_place(rr, f):
        n = rr * FIELDS + f
        return n // 18, HALO * (n % 9) + 64 * (n % 18 // 9)

    slabs = [jnp.zeros((CR, 128), jnp.float32)] * 3
    for rr in range(REFINE):
        for f in range(FIELDS):
            a, b = shares[rr] if f == SHARE else rows_of(f, rr)
            x = jnp.where(lane16 < HALO, a, jnp.where((lane16 >= 29) & (lane16 < 32), b, 0.0))
            n, at = slab_place(rr, f)
            slabs[n] = slabs[n] + (pltpu.roll(x, at, 1) if at else x)
    for n in range(3):
        hsend[n] = slabs[n]

    def sideways(n, j):
        return pltpu.make_async_remote_copy(
            src_ref=hsend,
            dst_ref=hrecv.at[n],
            send_sem=hs_sem.at[n],
            recv_sem=hr_sem.at[n],
            device_id=(mi, j),
            device_id_type=MESH,
        )

    @pl.when(has_left)
    def _():
        sideways(0, mj - 1).start()

    @pl.when(has_right)
    def _():
        sideways(1, mj + 1).start()

    for rr in range(REFINE):
        for f in range(SHARE):
            put(f, rr, halves(*rows_of(f, rr)))
        put(SHARE, rr, halves(*shares[rr]))

    def vertical(v, i):
        return pltpu.make_async_remote_copy(
            src_ref=vsend.at[v],
            dst_ref=vrecv.at[v],
            send_sem=vs_sem.at[v],
            recv_sem=vr_sem.at[v],
            device_id=(i, mj),
            device_id_type=MESH,
        )

    def corner(v, s, i, j):
        return pltpu.make_async_remote_copy(
            src_ref=csend.at[v, s],
            dst_ref=crecv.at[v, s],
            send_sem=cs_sem.at[v, s],
            recv_sem=cr_sem.at[v, s],
            device_id=(i, j),
            device_id_type=MESH,
        )

    incoming = 0
    for has, i, left, right, end in sides:
        incoming += has.astype(jnp.int32) + (has & left).astype(jnp.int32) + (has & right).astype(jnp.int32)
    incoming += nc * ((has_up & (mj == 0)).astype(jnp.int32) + (has_down & (mj == nc - 1)).astype(jnp.int32))

    @pl.when(jnp.logical_not(is_lead))
    def _():
        pl.semaphore_wait(barrier, incoming)

    @pl.when((mj == lead - 1) | (mj == lead + 1))
    def _():
        pl.semaphore_signal(relay_sem, inc=1, device_id=(mi, lead), device_id_type=MESH)

    @pl.when(is_lead)
    def _():
        pl.semaphore_wait(relay_sem, 2)

    @pl.when(first_up)
    def _():
        @pl.loop(0, nc)
        def _(k):
            piece(k, mi - 1, CR, zh_sem, zr_sem.at[1]).start()

    @pl.when(last_down)
    def _():
        @pl.loop(0, nc)
        def _(k):
            piece(k, mi + 1, CR + 1, zh_sem, zr_sem.at[2]).start()

    for v, (has, i, left, right, end) in enumerate(sides):

        @pl.when(has)
        def _(v=v, i=i):
            vertical(v, i).start()

        @pl.when(has & left)
        def _(v=v, i=i):
            corner(v, 0, i, mj - 1).start()

        @pl.when(has & right)
        def _(v=v, i=i):
            corner(v, 1, i, mj + 1).start()

    for v, (has, i, left, right, end) in enumerate(sides):

        @pl.when(jnp.logical_not(has))
        def _(v=v):
            vrecv[1 - v] = jnp.zeros(vrecv.shape[1:], jnp.float32)

        @pl.when(jnp.logical_not(has & left))
        def _(v=v):
            crecv[1 - v, 1] = jnp.zeros((1, 128), jnp.float32)

        @pl.when(jnp.logical_not(has & right))
        def _(v=v):
            crecv[1 - v, 0] = jnp.zeros((1, 128), jnp.float32)

    @pl.when(jnp.logical_not(has_right))
    def _():
        hrecv[0] = jnp.zeros(hrecv.shape[1:], jnp.float32)

    @pl.when(jnp.logical_not(has_left))
    def _():
        hrecv[1] = jnp.zeros(hrecv.shape[1:], jnp.float32)

    def widen(groups):
        n = groups[0].shape[0]
        column = jnp.minimum(tenth(iota((n, 128), 1) + 7), 9)
        wide = []
        for f in range(COARSE):
            at = 24 * (f % 5)
            wide.append([take(groups[f // 5], column + (at + 8 * half)) for half in range(2)])
        return wide

    def layers_of(wide):
        por_w = wide[1]
        liquid, ice_w, room, per_pore = [], [], [], []
        for k in range(LAYERS):
            depth = 1000.0 * thickness[k]
            liquid.append(wide[2 + k] * depth)
            ice_w.append(wide[2 + LAYERS + k] * depth)
            room.append((por_w - wide[2 + LAYERS + k]) * depth)
            per_pore.append((math.sqrt(layer_speed[k]) / depth) / por_w)
        return liquid, ice_w, room, per_pore

    row_pieces().wait_recv()

    def rows_at(group, slots):
        return jnp.concatenate([zrecv[n, :, 128 * group : 128 * group + 128] for n in slots], 0)

    wide = [jnp.concatenate(x, 0) for x in widen([rows_at(g, range(CR)) for g in range(2)])]
    excess_w = wide[0]
    liquid_w, ice_w, room, per_pore = layers_of(wide)
    for n, x in enumerate(ice_w + room + per_pore):
        coarse[n] = x

    @pl.when(has_right)
    def _():
        sideways(0, mj).wait_recv()

    @pl.when(has_left)
    def _():
        sideways(1, mj).wait_recv()

    in_left = lane16 < HALO
    in_right = (lane16 >= 83) & (lane16 < 83 + HALO)
    for rr in range(REFINE):
        for f in range(FIELDS):
            n, at = slab_place(rr, f)
            from_left = pltpu.roll(hrecv[1, n], (-29 - at) % 128, 1)
            from_right = pltpu.roll(hrecv[0, n], (83 - at) % 128, 1)
            ref, off = field(f)
            r = off + rr * ROWS
            ref[r : r + CR] = jnp.where(in_left, from_left, ref[r : r + CR])
            ref[r + CR : r + ROWS] = jnp.where(in_right, from_right, ref[r + CR : r + ROWS])

    END = ROWS * (REFINE + 1)
    up_of = functools.partial(pltpu.roll, shift=1, axis=0)
    down_of = functools.partial(pltpu.roll, shift=ROWS - 1, axis=0)
    dirs[:ROWS] = up_of(dirs[END - ROWS : END])
    dirs[END:] = down_of(dirs[ROWS : 2 * ROWS])

    def finish_wrap(b):
        for f in range(FIELDS):
            moving[b, f, :ROWS] = up_of(moving[b, f, END - ROWS : END])
            moving[b, f, END:] = down_of(moving[b, f, ROWS : 2 * ROWS])

    def main_in(b, r, c):
        masks = inflow_masks(*[dirs[pl.ds(r + n * ROWS, CR), :] for n in range(3)])
        arriving = [
            inflow(masks, *[moving[b, f, pl.ds(r + n * ROWS, CR), :] for n in range(3)])
            for f in range(FIELDS)
        ]
        left = [rest[f, pl.ds(r, CR), :] for f in range(FIELDS)]
        return settle(left, arriving, [coarse[LAYERS + k, c : c + CR] for k in range(LAYERS)])

    def main_out(b, r, c, h, liquid):
        move, left, chan = outflow(
            h,
            liquid,
            stat[ORATE, pl.ds(r, CR), :],
            stat[KIND, pl.ds(r, CR), :],
            stat[LRATE, pl.ds(r, CR), :],
            [coarse[k, c : c + CR] for k in range(LAYERS)],
            [coarse[2 * LAYERS + k, c : c + CR] for k in range(LAYERS)],
        )
        for f in range(FIELDS):
            moving[b, f, pl.ds(r + ROWS, CR), :] = move[f]
            rest[f, pl.ds(r, CR), :] = left[f]
        return chan

    def row_at(rr, c):
        return pl.multiple_of(rr * ROWS + c, CR)

    zero16 = jnp.zeros((CR, 128), jnp.float32)

    def first(rr, chan):
        out = []
        for n, c in enumerate((0, CR)):
            r = row_at(rr, c)
            h = excess_w[c : c + CR] * stat[SHARE, pl.ds(r, CR), :]
            out.append(chan[n] + main_out(0, r, c, h, [x[c : c + CR] for x in liquid_w]))
        return tuple(out)

    chan = lax.fori_loop(0, REFINE, first, (zero16, zero16), unroll=2)
    finish_wrap(0)

    for b in range(2):

        def middle(rr, chan, b=b):
            out = []
            for n, c in enumerate((0, CR)):
                r = row_at(rr, c)
                out.append(chan[n] + main_out(1 - b, r, c, *main_in(b, r, c)))
            return tuple(out)

        chan = lax.fori_loop(0, REFINE, middle, chan, unroll=2)
        finish_wrap(1 - b)

    def last(rr, sums):
        out = []
        for n, c in enumerate((0, CR)):
            h, liquid = main_in(0, row_at(rr, c), c)
            out.append(tuple(a + x for a, x in zip(sums[n], liquid + [h])))
        return tuple(out)

    sums = lax.fori_loop(0, REFINE, last, ((zero16,) * (LAYERS + 1),) * 2, unroll=2)

    row_p, col_p = iota((128, 128), 0), iota((128, 128), 1)
    inside = (row_p >= HALO) & (row_p < HALO + 80)
    to_block = jnp.where((tenth(row_p + 7) == col_p + 1) & inside, 1.0, 0.0).astype(jnp.bfloat16)
    scales = [0.01 / (1000.0 * x) for x in thickness] + [0.01, 0.01]
    blocks = [x * scales[n] for half in range(2) for n, x in enumerate(sums[half] + (chan[half],))]
    means = dot2(jnp.concatenate(blocks, 0), to_block)
    back = jnp.zeros((CR, 128), jnp.float32)
    for half in range(2):
        for n in range(LAYERS + 2):
            r = (half * (LAYERS + 2) + n) * CR
            at = 16 * n + 8 * half
            back = back + (pltpu.roll(means[r : r + CR], at, 1) if at else means[r : r + CR])
    for s in range(1, CR - 1):
        bsend[s] = back[s : s + 1]

    def answer(k, s):
        return pltpu.make_async_remote_copy(
            src_ref=bsend.at[k],
            dst_ref=brecv.at[s],
            send_sem=bs_sem,
            recv_sem=br_sem,
            device_id=(mi, k),
            device_id_type=MESH,
        )

    def answers():
        return pltpu.make_async_remote_copy(
            src_ref=bsend.at[: nc - 1],
            dst_ref=brecv.at[: nc - 1],
            send_sem=bs_sem,
            recv_sem=br_sem,
            device_id=(mi, mj),
            device_id_type=MESH,
        )

    for k in others(mj):

        @pl.when((k != 0) & (k != nc - 1))
        def _(k=k):
            answer(k, mj).start()

    for v, (has, i, left, right, end) in enumerate(sides):

        @pl.when(has)
        def _(v=v):
            vertical(1 - v, mi).wait_recv()

        @pl.when(has & left)
        def _(v=v):
            corner(1 - v, 1, mi, mj).wait_recv()

        @pl.when(has & right)
        def _(v=v):
            corner(1 - v, 0, mi, mj).wait_recv()

    @pl.when(has_down)
    def _():
        piece(0, mi, CR, zh_sem, zr_sem.at[1]).wait_recv()

    @pl.when(has_up)
    def _():
        piece(0, mi, CR + 1, zh_sem, zr_sem.at[2]).wait_recv()

    for v in range(2):
        for half, mine in enumerate((in_left, in_right)):
            index = jnp.clip(HALO * iota((CR, 128), 0) + lane16 - 83 * half, 0, 127)
            side = take(jnp.broadcast_to(crecv[v, 1 - half], (CR, 128)), index)
            vrecv[v, half] = jnp.where(mine, side, vrecv[v, half])
    for f in range(FIELDS):
        ref, off = field(f)
        for half in range(2):
            for v in range(2):
                r = (2 * v + half) * CR
                own = off + half * CR
                if v == 0:
                    own_rows = ref[pl.ds(own, REFINE, stride=ROWS), :]
                    next_rows = ref[pl.ds(own + 1, HALO, stride=ROWS), :]
                    at, near = r, r + HALO + REFINE
                else:
                    own_rows = ref[pl.ds(own + CR - 1, REFINE, stride=ROWS), :]
                    next_rows = ref[pl.ds(own + (REFINE - HALO) * ROWS + CR - 2, HALO, stride=ROWS), :]
                    at, near = r + HALO + REFINE, r
                sstat[f, r + HALO : r + HALO + REFINE] = own_rows
                sstat[f, near : near + HALO] = next_rows
                sstat[f, at : at + HALO] = vrecv[1 - v, half, HALO * f : HALO * f + HALO]
    sub8 = iota((8, 128), 0)

    def strip_rows(group):
        def row(n):
            return jnp.broadcast_to(zrecv[n, :, 128 * group : 128 * group + 128], (8, 128))

        return [
            jnp.where(sub8 < 3, row(CR + 1), row(0)),
            jnp.where(sub8 < 5, row(0), row(1)),
            jnp.where(sub8 < 3, row(CR - 2), row(CR - 1)),
            jnp.where(sub8 < 5, row(CR - 1), row(CR)),
        ]

    groups = [jnp.concatenate(strip_rows(g), 0) for g in range(2)]
    wide = [jnp.concatenate([a[:CR], b[:CR], a[CR:], b[CR:]], 0) for a, b in widen(groups)]
    excess_w = wide[0]
    liquid, ice_w, room, per_pore = layers_of(wide)
    for n, x in enumerate(ice_w + room + per_pore):
        scoarse[n] = x
    sdir = sstat[DIR]
    sub_up = functools.partial(pltpu.roll, shift=1, axis=0)
    sub_down = functools.partial(pltpu.roll, shift=4 * CR - 1, axis=0)
    masks = inflow_masks(sub_up(sdir), sdir, sub_down(sdir))
    h = excess_w * sstat[SHARE]
    chan = jnp.zeros((4 * CR, 128), jnp.float32)
    for step in range(3):
        move, left, taken = outflow(
            h,
            liquid,
            sstat[ORATE],
            sstat[KIND],
            sstat[LRATE],
            [scoarse[k] for k in range(LAYERS)],
            [scoarse[2 * LAYERS + k] for k in range(LAYERS)],
        )
        chan = chan + taken
        arriving = [inflow(masks, sub_up(m), m, sub_down(m)) for m in move]
        h, liquid = settle(left, arriving, [scoarse[LAYERS + k] for k in range(LAYERS)])

    sub16 = iota((CR, 128), 0)
    of_row = (sub16 >= HALO) & (sub16 < HALO + REFINE)
    sums = []
    for v in range(2):
        for n, x in enumerate(liquid + [h, chan]):
            for half in range(2):
                r = (2 * v + half) * CR
                sums.append(jnp.sum(jnp.where(of_row, x[r : r + CR], 0.0), 0, keepdims=True) * scales[n])
        sums.append(jnp.zeros((4, 128), jnp.float32))
    means = dot2(jnp.concatenate(sums, 0), to_block)
    for v in range(2):
        x = pltpu.roll(means[v * CR : (v + 1) * CR], 0, 1, stride=8, stride_axis=0)
        bsend[v * (CR - 1)] = jnp.sum(x, 0, keepdims=True)

    for k in (0, nc - 1):

        @pl.when(mj != k)
        def _(k=k):
            answer(k, mj).start()

    brecv[mj] = bsend[mj]

    row_pieces().wait_send()

    @pl.when(first_up | last_down)
    def _():
        pltpu.make_async_remote_copy(
            src_ref=zsend,
            dst_ref=zrecv.at[:nc],
            send_sem=zh_sem,
            recv_sem=zr_sem.at[1],
            device_id=(mi, mj),
            device_id_type=MESH,
        ).wait_send()

    for v, (has, i, left, right, end) in enumerate(sides):

        @pl.when(has)
        def _(v=v, i=i):
            vertical(v, i).wait_send()

        @pl.when(has & left)
        def _(v=v, i=i):
            corner(v, 0, i, mj - 1).wait_send()

        @pl.when(has & right)
        def _(v=v, i=i):
            corner(v, 1, i, mj + 1).wait_send()

    @pl.when(has_left)
    def _():
        sideways(0, mj - 1).wait_send()

    @pl.when(has_right)
    def _():
        sideways(1, mj + 1).wait_send()

    answers().wait_recv()

    gather = jnp.minimum(iota((8, 128), 0) * 16 + (lane & 15), 127)
    owner = lax.shift_right_logical(lane, 4)
    for half in range(2):
        out = jnp.zeros((8, 128), jnp.float32)
        for s in range(8):
            x = jnp.broadcast_to(brecv[8 * half + s], (8, 128))
            out = jnp.where(owner == s, take(x, gather), out)
        lanes = slice(128 * half, 128 * half + 128)
        for k in range(LAYERS):
            out_liq[k, :, lanes] = out[k : k + 1]
        out_h[:, lanes] = out[LAYERS : LAYERS + 1]
        out_c[:, lanes] = out[LAYERS + 1 : LAYERS + 2]

    answers().wait_send()


def store(a, b, c, out_a, out_b, out_c, sem):
    copies = [
        pltpu.make_async_copy(src, dst, sem.at[n])
        for n, (src, dst) in enumerate(((a, out_a), (b, out_b), (c, out_c)))
    ]
    for copy in copies:
        copy.start()
    for copy in copies:
        copy.wait()


def solution(mesh):
    nr, nc = mesh.shape["rows"], mesh.shape["cols"]
    f32, bf16 = jnp.float32, jnp.bfloat16

    def step(*args):
        v = pltpu.VMEM
        dma = pltpu.SemaphoreType.DMA
        args = [pltpu.with_memory_space_constraint(x, pltpu.HBM) for x in args]
        results = pl.pallas_call(
            functools.partial(kernel, nr, nc),
            out_shape=(v((LAYERS, 1, W), f32), v((1, W), f32), v((1, W), f32)),
            in_specs=[pl.BlockSpec(memory_space=pltpu.HBM)] * 10,
            out_specs=[pl.BlockSpec(memory_space=pltpu.VMEM)] * 3,
            scratch_shapes=[
                v((1, W), f32),
                v((1, W), f32),
                v((1, W), f32),
                v((LAYERS, 1, W), f32),
                v((LAYERS, 1, W), f32),
                v((TILE, TILE), jnp.int32),
                v((TILE, TILE), jnp.int32),
                v((TILE, TILE), bf16),
                v((TILE, TILE), bf16),
                v((TILE, TILE), bf16),
                v((2 * FIELDS, TILE, 128), f32),
                v((FIELDS, 2 * TILE, 128), f32),
                v((2 * TILE + 2 * ROWS, 128), f32),
                v((3 * LAYERS, ROWS, 128), f32),
                v((2, FIELDS, 2 * TILE + 2 * ROWS, 128), f32),
                v((FIELDS, 2 * TILE, 128), f32),
                v((FIELDS, 4 * CR, 128), f32),
                v((3 * LAYERS, 4 * CR, 128), f32),
                v((CR, 1, W), f32),
                v((CR + 2, 1, W), f32),
                v((2, 2, CR, 128), f32),
                v((2, 2, CR, 128), f32),
                v((2, 2, 1, 128), f32),
                v((2, 2, 1, 128), f32),
                v((3, CR, 128), f32),
                v((2, 3, CR, 128), f32),
                v((CR, 1, 128), f32),
                v((CR, 1, 128), f32),
                dma((10,)),
                dma(()),
                dma(()),
                dma((3,)),
                dma((2,)),
                dma((2,)),
                dma((2, 2)),
                dma((2, 2)),
                dma((2,)),
                dma((2,)),
                dma(()),
                dma(()),
                pltpu.SemaphoreType.REGULAR,
                pltpu.SemaphoreType.REGULAR,
            ],
            compiler_params=pltpu.CompilerParams(
                collective_id=0, has_side_effects=True, vmem_limit_bytes=62 * 1024 * 1024
            ),
        )(*args)
        return pl.pallas_call(
            store,
            out_shape=(
                jax.ShapeDtypeStruct((LAYERS, 1, W), f32),
                jax.ShapeDtypeStruct((1, W), f32),
                jax.ShapeDtypeStruct((1, W), f32),
            ),
            in_specs=[pl.BlockSpec(memory_space=pltpu.VMEM)] * 3,
            out_specs=[pl.BlockSpec(memory_space=pltpu.HBM)] * 3,
            scratch_shapes=[dma((3,))],
        )(*[pltpu.with_memory_space_constraint(x, pltpu.VMEM) for x in results])

    return jax.shard_map(
        step,
        mesh=mesh,
        in_specs=(
            P(("rows", "cols"), None),
            P(("rows", "cols"), None),
            P(("rows", "cols"), None),
            P(None, ("rows", "cols"), None),
            P(None, ("rows", "cols"), None),
            P("rows", "cols"),
            P("rows", "cols"),
            P("rows", "cols"),
            P("rows", "cols"),
            P("rows", "cols"),
        ),
        out_specs=(
            P(None, ("rows", "cols"), None),
            P(("rows", "cols"), None),
            P(("rows", "cols"), None),
        ),
        check_vma=False,
    )
```

time: 35.2 us -> 20.7 us (0.59)
  local copies, waits for them, and re-layouts: 9.61 us -> 0 us
  Pallas kernels: 24.5 us -> 20 us
    unnamed x23 -> x0, local copies, waits for them, and re-layouts: 9.61 us -> none
    pallas_call x1 -> x2, Pallas kernels: 24.5 us -> 20 us  [the longest x1 19.4 us: step(): pl.pallas_call(functools.partial(kernel, nr, nc), out_shape=(v((LAYERS, 1...]
where the time goes in v2:
time: 20.7 us; the launch traced here: 20.6 us
  Pallas kernels  20 us (97%)
  between operations  0.64 us (3%)
    pallas_call x1, Pallas kernels, step(): pl.pallas_call(functools.partial(kernel, nr, nc), out_shape=(v((LAYERS, 1...  19.4 us
    pallas_call x1, Pallas kernels, step(): pl.pallas_call(store, out_shape=(jax.ShapeDtypeStruct((LAYERS, 1, W), f32...  0.63 us

profile of v2, /device:TPU:6, one launch (start us, length us, event | category | flops | bytes accessed | tf_op | source)
XLA Modules:
  0.0 20.6 jit_solution(9223469219870257142)
XLA Ops:
  0.6 19.4 %shard_map.121 = (f32[4,1,256]{2,1,0:T(1,128)S(1)}, f32[1,256]{1,0:T(1,128)S(1)}, f32[1,256]{1,0:T(1,128)S(1)}) custom-call(f32[1,256]{1,0:T(1,128)} %rain_h.1, f32[1,256]{1,0:T(1,128)} %infil_h.1, f32[1,256]{1,0:T(1,128)} %por_h.1, f32[4,1,256]{2,1,0:T(1,128)} %liq_h.1, f32[4,1,256]{2,1,0:T(1,128)} %ice_h.1, s32[160,160]{1,0:T(8,128)} %dir_h.1, ...), custom_call_target="tpu_custom_call" | custom-call | tf_op jit(solution)/shard_map/pallas_call | solution.py:836
  20.0 0.6 %shard_map.122 = (f32[4,1,256]{2,1,0:T(1,128)}, f32[1,256]{1,0:T(1,128)}, f32[1,256]{1,0:T(1,128)}) custom-call(f32[4,1,256]{2,1,0:T(1,128)S(1)} %get-tuple-element.6.a, f32[1,256]{1,0:T(1,128)S(1)} %get-tuple-element.7.b, f32[1,256]{1,0:T(1,128)S(1)} %get-tuple-element.8.c), custom_call_target="tpu_custom_call" | custom-call | tf_op jit(solution)/shard_map/pallas_call | solution.py:889

commit v3 on v2

v3 whole, which is shorter than its diff:
```python
import functools
import math

import jax
import jax.numpy as jnp
from jax import lax
from jax.experimental import pallas as pl
from jax.experimental.pallas import tpu as pltpu
from jax.sharding import PartitionSpec as P

MESH = pl.DeviceIdType.MESH
REFINE = 10
LAYERS = 4
TILE = 160
CR = 16
W = 256
HALO = 3
PAIRS = REFINE // 2
ROWS = 3 * CR
SPLIT = 56

thickness = (0.1, 0.3, 0.6, 1.0)
layer_speed = (1.0, 0.8, 0.6, 0.4)

DIR, ORATE, LAND, LRATE, SHARE, CHANNEL = range(6)
FIELDS = 5
COARSE = 10


FAR_FIRST = sorted(
    ((z, y, c) for z in range(2) for y in range(4) for c in range(2) if z + y + c),
    key=lambda p: -(p[0] + min(p[1], 4 - p[1])),
)


def others(j):
    z, y, c = j // 8, (j // 2) % 4, j % 2
    return [((z + dz) % 2) * 8 + ((y + dy) % 4) * 2 + (c + dc) % 2 for dz, dy, dc in FAR_FIRST]


def iota(shape, dim):
    return lax.broadcasted_iota(jnp.int32, shape, dim)


def take(x, index):
    return jnp.take_along_axis(x, index, axis=1, mode="promise_in_bounds")


def tenth(x):
    return lax.shift_right_logical(x * 6554, 16)


def split3(x):
    hi = x.astype(jnp.bfloat16)
    r = x - hi.astype(jnp.float32)
    mid = r.astype(jnp.bfloat16)
    lo = (r - mid.astype(jnp.float32)).astype(jnp.bfloat16)
    return jnp.concatenate([hi, mid, lo], 0)


def split2(x):
    hi = x.astype(jnp.bfloat16)
    lo = (x - hi.astype(jnp.float32)).astype(jnp.bfloat16)
    return jnp.concatenate([hi, lo], 0)


def dot3(x, ones):
    n = x.shape[0]
    y = jnp.dot(split3(x), ones, preferred_element_type=jnp.float32)
    return y[:n] + y[n : 2 * n] + y[2 * n :]


def dot2(x, ones):
    n = x.shape[0]
    y = jnp.dot(split2(x), ones, preferred_element_type=jnp.float32)
    return y[:n] + y[n:]


def inflow_masks(d_up, d_mid, d_down):
    return (
        d_up == 1.0,
        d_mid == 0.0,
        d_down == 7.0,
        d_up == 3.0,
        d_mid == 4.0,
        d_down == 5.0,
        d_up == 2.0,
        d_down == 6.0,
    )


def inflow(masks, up, mid, down):
    e0, e1, e2, w0, w1, w2, s0, s1 = masks
    zero = jnp.zeros_like(up)
    east = jnp.where(e0, up, zero) + jnp.where(e1, mid, zero) + jnp.where(e2, down, zero)
    west = jnp.where(w0, up, zero) + jnp.where(w1, mid, zero) + jnp.where(w2, down, zero)
    same = jnp.where(s0, up, zero) + jnp.where(s1, down, zero)
    return same + pltpu.roll(east, 1, 1) + pltpu.roll(west, 127, 1)


def outflow(h, liquid, orate, land, channel, lrate, ice, per_pore):
    q = orate * h * (h / (h + 2.0))
    moving = [q * land]
    rest = [h - q]
    for k in range(LAYERS):
        sat = jnp.minimum((liquid[k] + ice[k]) * per_pore[k], math.sqrt(layer_speed[k]))
        lateral = (lrate * liquid[k]) * (sat * sat)
        moving.append(lateral)
        rest.append(liquid[k] - lateral)
    return moving, rest, q * channel


def settle(rest, arriving, room):
    h = rest[0] + arriving[0]
    liquid = []
    for k in range(LAYERS):
        u = rest[1 + k] + arriving[1 + k]
        h = h + jnp.maximum(u - room[k], 0.0)
        liquid.append(jnp.minimum(u, room[k]))
    return h, liquid


def kernel(
    nr,
    nc,
    rain_h,
    infil_h,
    por_h,
    liq_h,
    ice_h,
    dir_h,
    kind_h,
    orate_h,
    lrate_h,
    weight_h,
    out_liq,
    out_h,
    out_c,
    rain,
    infil,
    por,
    liq,
    ice,
    dir_v,
    kind_v,
    orate_v,
    lrate_v,
    weight_v,
    nat,
    share_v,
    stat,
    dirs,
    coarse,
    moving,
    rest,
    sums,
    sstat,
    schannel,
    enter,
    zsend,
    zrecv,
    vsend,
    vrecv,
    csend,
    crecv,
    hsend,
    hrecv,
    bsend,
    brecv,
    in_sem,
    zs_sem,
    zh_sem,
    zr_sem,
    vs_sem,
    vr_sem,
    cs_sem,
    cr_sem,
    hs_sem,
    hr_sem,
    bs_sem,
    br_sem,
    row_sem,
    relay_sem,
):
    mi = lax.axis_index("rows")
    mj = lax.axis_index("cols")
    has_up, has_down = mi > 0, mi < nr - 1
    has_left, has_right = mj > 0, mj < nc - 1

    barrier = pltpu.get_barrier_semaphore()
    lead = nc - 2
    is_lead = mj == lead

    def tell(i, j):
        pl.semaphore_signal(barrier, inc=1, device_id=(i, j), device_id_type=MESH)

    @pl.when(jnp.logical_not(is_lead))
    def _():
        tell(mi, lead)

    copies = [
        pltpu.make_async_copy(src, dst, in_sem.at[n])
        for n, (src, dst) in enumerate(
            (
                (rain_h, rain),
                (infil_h, infil),
                (por_h, por),
                (liq_h, liq),
                (ice_h, ice),
                (weight_h, weight_v),
                (dir_h, dir_v),
                (kind_h, kind_v),
                (orate_h, orate_v),
                (lrate_h, lrate_v),
            )
        )
    ]
    for copy in copies:
        copy.start()

    sides = (
        (has_up, mi - 1, has_left, has_right, nc - 1),
        (has_down, mi + 1, has_left, has_right, 0),
    )
    for has, i, left, right, end in sides:

        @pl.when(has)
        def _(i=i, end=end):
            tell(i, end)

        @pl.when(has & jnp.logical_not(is_lead))
        def _(i=i):
            tell(i, mj)

        @pl.when(has & left & (mj - 1 != lead))
        def _(i=i):
            tell(i, mj - 1)

        @pl.when(has & right & (mj + 1 != lead))
        def _(i=i):
            tell(i, mj + 1)

    @pl.when(is_lead)
    def _():
        pl.semaphore_wait(barrier, nc - 1)
        for k in range(nc):
            if k != lead:
                pl.semaphore_signal(row_sem, inc=1, device_id=(mi, k), device_id_type=MESH)

    lane = iota((8, 128), 1)
    lane16 = iota((CR, 128), 1)
    sub16 = iota((CR, 128), 0)

    def piece(k, i, s, send, arrive):
        return pltpu.make_async_remote_copy(
            src_ref=zsend.at[k],
            dst_ref=zrecv.at[s],
            send_sem=send,
            recv_sem=arrive,
            device_id=(i, k),
            device_id_type=MESH,
        )

    def row_pieces():
        return pltpu.make_async_remote_copy(
            src_ref=zsend.at[: nc - 1],
            dst_ref=zrecv.at[: nc - 1],
            send_sem=zs_sem,
            recv_sem=zr_sem.at[0],
            device_id=(mi, mj),
            device_id_type=MESH,
        )

    first_up = has_up & (mj == 0)
    last_down = has_down & (mj == nc - 1)

    def first_run(a):
        return pltpu.roll(a, HALO, 1)

    def second_run(a, b):
        return jnp.where(lane16 < 21, pltpu.roll(a, 21, 1), pltpu.roll(b, 21, 1))

    def third_run(a):
        return pltpu.roll(a, 59, 1)

    def fourth_run(a, b):
        return jnp.where(lane16 < 81, pltpu.roll(a, 81, 1), pltpu.roll(b, 81, 1))

    def rows_of(f, rr):
        return [nat.at[2 * f + half][pl.ds(rr, CR, stride=REFINE), :] for half in range(2)]

    def field(f):
        return (dirs, ROWS) if f == DIR else (stat.at[f], 0)

    def vertical(v, i):
        return pltpu.make_async_remote_copy(
            src_ref=vsend.at[v],
            dst_ref=vrecv.at[v],
            send_sem=vs_sem.at[v],
            recv_sem=vr_sem.at[v],
            device_id=(i, mj),
            device_id_type=MESH,
        )

    def corner(v, s, i, j):
        return pltpu.make_async_remote_copy(
            src_ref=csend.at[v, s],
            dst_ref=crecv.at[v, s],
            send_sem=cs_sem.at[v, s],
            recv_sem=cr_sem.at[v, s],
            device_id=(i, j),
            device_id_type=MESH,
        )

    incoming = 0
    for has, i, left, right, end in sides:
        incoming += has.astype(jnp.int32) + (has & left).astype(jnp.int32) + (has & right).astype(jnp.int32)
    incoming += nc * ((has_up & (mj == 0)).astype(jnp.int32) + (has_down & (mj == nc - 1)).astype(jnp.int32))

    def rows_ready():
        @pl.when(jnp.logical_not(is_lead))
        def _():
            pl.semaphore_wait(barrier, incoming)

        @pl.when((mj == lead - 1) | (mj == lead + 1))
        def _():
            pl.semaphore_signal(relay_sem, inc=1, device_id=(mi, lead), device_id_type=MESH)

        @pl.when(is_lead)
        def _():
            pl.semaphore_wait(relay_sem, 2)

    def send_ends():
        @pl.when(first_up)
        def _():
            @pl.loop(0, nc)
            def _(k):
                piece(k, mi - 1, CR, zh_sem, zr_sem.at[1]).start()

        @pl.when(last_down)
        def _():
            @pl.loop(0, nc)
            def _(k):
                piece(k, mi + 1, CR + 1, zh_sem, zr_sem.at[2]).start()

    def send_rows():
        for v, (has, i, left, right, end) in enumerate(sides):

            @pl.when(has)
            def _(v=v, i=i):
                vertical(v, i).start()

            @pl.when(has & left)
            def _(v=v, i=i):
                corner(v, 0, i, mj - 1).start()

            @pl.when(has & right)
            def _(v=v, i=i):
                corner(v, 1, i, mj + 1).start()

    def coarse_part():
        for copy in copies[:5]:
            copy.wait()
        rain_x, por_x = rain[...], por[...]
        top_sat = (liq[0] + ice[0]) / por_x
        capacity = infil[...] * jnp.maximum(1.0 - top_sat, 0.1)
        excess = rain_x * rain_x / (rain_x + capacity)
        top = liq[0] + (rain_x - excess) / (1000.0 * thickness[0])
        strip = [excess, por_x, top] + [liq[k] for k in range(1, LAYERS)] + [ice[k] for k in range(LAYERS)]

        slot = lax.shift_right_logical(lane * 2731, 16)
        t = lane - slot * 24
        for half in range(2):
            base = (iota((8, 128), 0) + 8 * half) * 16 - 1 + t
            inside = jnp.clip(base, 0, W - 1)
            index = inside & 127
            low = inside < 128
            for group in range(2):
                packed = jnp.zeros((8, 128), jnp.float32)
                for n in range(5):
                    x = strip[group * 5 + n]
                    a = jnp.broadcast_to(x[:, :128], (8, 128))
                    b = jnp.broadcast_to(x[:, 128:], (8, 128))
                    packed = jnp.where(slot == n, jnp.where(low, take(a, index), take(b, index)), packed)
                for s in range(8):
                    zsend[8 * half + s, :, 128 * group : 128 * group + 128] = packed[s : s + 1]

        zrecv[mj] = zsend[mj]

        @pl.when(jnp.logical_not(has_down))
        def _():
            zrecv[CR] = zsend[mj]

        @pl.when(jnp.logical_not(has_up))
        def _():
            zrecv[CR + 1] = zsend[mj]

    def tile_part():
        for copy in copies[5:]:
            copy.wait()
        kind_x = kind_v[...]
        natural = (
            dir_v[...].astype(jnp.float32),
            jnp.where(kind_x == 2, 0.0, orate_v[...].astype(jnp.float32)),
            jnp.where(kind_x == 0, 1.0, 0.0),
            lrate_v[...].astype(jnp.float32),
            weight_v[...].astype(jnp.float32),
            jnp.where(kind_x == 1, 1.0, 0.0),
        )
        no_lanes = jnp.zeros((TILE, 96), jnp.float32)
        for f in range(FIELDS + 1):
            nat[2 * f] = natural[f][:, :128]
            nat[2 * f + 1] = jnp.concatenate([natural[f][:, 128:], no_lanes], 1)

        weights = [rows_of(SHARE, rr) for rr in range(REFINE)]
        total = [functools.reduce(lambda a, b: a + b, [w[half] for w in weights]) for half in range(2)]
        row_c, col_c = iota((W, W), 0), iota((W, W), 1)
        same_block = (tenth(row_c) == tenth(col_c)) & (row_c < TILE) & (col_c < TILE)
        block_sum = dot3(jnp.concatenate(total, 1), jnp.where(same_block, 1.0, 0.0).astype(jnp.bfloat16))
        per_mean = 100.0 / jnp.where(iota((CR, W), 1) < TILE, block_sum, 1.0)
        shares = [[w[half] * per_mean[:, 128 * half : 128 * half + 128] for half in range(2)] for w in weights]
        for rr in range(REFINE):
            for half in range(2):
                share_v[2 * rr + half] = shares[rr][half]

        place = lane16 - HALO * sub16
        for v in range(2):
            r = v * (TILE - HALO)
            for half in range(2):
                for f in range(SHARE):
                    vsend[v, half, HALO * f : HALO * f + HALO] = nat[2 * f + half, r : r + HALO]
                for p in range(HALO):
                    x = shares[p + v * (REFINE - HALO)][half][v * (CR - 1) : v * (CR - 1) + 1]
                    vsend[v, half, HALO * SHARE + p : HALO * SHARE + p + 1] = x
                vsend[v, half, HALO * FIELDS :] = jnp.zeros((1, 128), jnp.float32)
            a, b = vsend[v, 0], vsend[v, 1]
            if v == 0:
                vsend[v, 0], vsend[v, 1] = third_run(a), fourth_run(a, b)
            else:
                vsend[v, 0], vsend[v, 1] = first_run(a), second_run(a, b)
            for n, (x, at) in enumerate(((a, 0), (b, 29))):
                end = jnp.where((place >= 0) & (place < HALO), take(x, jnp.clip(place + at, 0, 127)), 0.0)
                csend[v, n] = jnp.sum(end, 0, keepdims=True)

    late = (lax.rem(mi, 4) == 3) & has_down
    late_first = late.astype(jnp.int32)

    @pl.loop(0, 2)
    def _(phase):
        part = lax.rem(phase + late_first, 2)

        @pl.when(part == 0)
        def _():
            coarse_part()

        @pl.when(part == 1)
        def _():
            tile_part()

        @pl.when((phase == 0) & jnp.logical_not(is_lead))
        def _():
            pl.semaphore_wait(row_sem, 1)

        @pl.when(part == 0)
        def _():
            for k in others(mj):
                piece(k, mi, mj, zs_sem, zr_sem.at[0]).start()

        @pl.when((part == 1) & late)
        def _():
            rows_ready()
            send_rows()

    @pl.when(late)
    def _():
        send_ends()

    shares = [[share_v[2 * rr + half] for half in range(2)] for rr in range(REFINE)]

    def slab_place(rr, f):
        n = rr * FIELDS + f
        return n // 18, HALO * (n % 9) + 64 * (n % 18 // 9)

    slabs = [jnp.zeros((CR, 128), jnp.float32)] * 3
    for rr in range(REFINE):
        for f in range(FIELDS):
            a, b = shares[rr] if f == SHARE else rows_of(f, rr)
            x = jnp.where(lane16 < HALO, a, jnp.where((lane16 >= 29) & (lane16 < 32), b, 0.0))
            n, at = slab_place(rr, f)
            slabs[n] = slabs[n] + (pltpu.roll(x, at, 1) if at else x)
    for n in range(3):
        hsend[n] = slabs[n]

    def sideways(n, j):
        return pltpu.make_async_remote_copy(
            src_ref=hsend,
            dst_ref=hrecv.at[n],
            send_sem=hs_sem.at[n],
            recv_sem=hr_sem.at[n],
            device_id=(mi, j),
            device_id_type=MESH,
        )

    @pl.when(has_left)
    def _():
        sideways(0, mj - 1).start()

    @pl.when(has_right)
    def _():
        sideways(1, mj + 1).start()

    for p in range(PAIRS):
        for f in range(FIELDS + 1):
            if f == SHARE:
                (a, b), (c, d) = shares[p], shares[p + PAIRS]
            else:
                (a, b), (c, d) = rows_of(f, p), rows_of(f, p + PAIRS)
            ref, off = field(f)
            r = off + p * ROWS
            ref[r : r + CR] = first_run(a)
            ref[r + CR : r + 2 * CR] = jnp.where(lane16 < SPLIT, second_run(a, b), third_run(c))
            ref[r + 2 * CR : r + ROWS] = fourth_run(c, d)

    def strip_own(f, v, out):
        ref, off = field(f)
        for half in range(2):
            at = 8 * half + (0 if v else HALO)
            r = off + (v + half) * CR + v * (CR - 1)
            out[at : at + PAIRS] = ref[pl.ds(r, PAIRS, stride=ROWS), :]

    lane8, sub8 = iota((8, 128), 1), iota((8, 128), 0)
    schannel[...] = jnp.zeros(schannel.shape, jnp.float32)
    for v in range(2):
        strip_own(CHANNEL, v, schannel.at[v])

    row48, lane48 = iota((ROWS, 128), 0), iota((ROWS, 128), 1)
    in_first = (row48 == 0) | ((row48 == CR) & (lane48 < SPLIT))
    in_last = (row48 == ROWS - 1) | ((row48 == 2 * CR - 1) & (lane48 >= SPLIT))
    for p in range(PAIRS):
        out = in_first if p < 2 else in_last if p > 2 else in_first | in_last
        r = p * ROWS
        stat[CHANNEL, r : r + ROWS] = jnp.where(out, 0.0, stat[CHANNEL, r : r + ROWS])

    @pl.when(jnp.logical_not(late))
    def _():
        rows_ready()
        send_ends()
        send_rows()

    for v, (has, i, left, right, end) in enumerate(sides):

        @pl.when(jnp.logical_not(has))
        def _(v=v):
            vrecv[1 - v] = jnp.zeros(vrecv.shape[1:], jnp.float32)

        @pl.when(jnp.logical_not(has & left))
        def _(v=v):
            crecv[1 - v, 1] = jnp.zeros((1, 128), jnp.float32)

        @pl.when(jnp.logical_not(has & right))
        def _(v=v):
            crecv[1 - v, 0] = jnp.zeros((1, 128), jnp.float32)

    @pl.when(jnp.logical_not(has_right))
    def _():
        hrecv[0] = jnp.zeros(hrecv.shape[1:], jnp.float32)

    @pl.when(jnp.logical_not(has_left))
    def _():
        hrecv[1] = jnp.zeros(hrecv.shape[1:], jnp.float32)

    def columns(n):
        lanes = iota((n, 128), 1)
        return (
            tenth(lanes + 7),
            tenth(jnp.where(lanes < SPLIT, lanes + 117, lanes - 49)),
            jnp.minimum(tenth(lanes + 57), 17),
        )

    def layers_of(wide):
        por_w = wide[1]
        liquid, ice_w, room, per_pore = [], [], [], []
        for k in range(LAYERS):
            depth = 1000.0 * thickness[k]
            liquid.append(wide[2 + k] * depth)
            ice_w.append(wide[2 + LAYERS + k] * depth)
            room.append((por_w - wide[2 + LAYERS + k]) * depth)
            per_pore.append((math.sqrt(layer_speed[k]) / depth) / por_w)
        return liquid, ice_w, room, per_pore

    row_pieces().wait_recv()

    def rows_at(group, slots):
        return jnp.concatenate([zrecv[n, :, 128 * group : 128 * group + 128] for n in slots], 0)

    packed_rows = [rows_at(g, range(CR)) for g in range(2)]
    wide = [
        jnp.concatenate([take(packed_rows[f // 5], c + 24 * (f % 5)) for c in columns(CR)], 0) for f in range(COARSE)
    ]
    liquid_w, ice_w, room, per_pore = layers_of(wide)
    for n, x in enumerate(ice_w + room + per_pore + liquid_w + wide[:1]):
        coarse[n] = x

    @pl.when(has_right)
    def _():
        sideways(0, mj).wait_recv()

    @pl.when(has_left)
    def _():
        sideways(1, mj).wait_recv()

    def span(at):
        return (lane16 >= at) & (lane16 < at + HALO)

    for p in range(PAIRS):
        for f in range(FIELDS):
            ref, off = field(f)
            r = off + p * ROWS
            for rr, (left_row, left_at), (right_row, right_at) in (
                (p, (r, 0), (r + CR, SPLIT - HALO)),
                (p + PAIRS, (r + CR, SPLIT), (r + 2 * CR, 113)),
            ):
                n, at = slab_place(rr, f)
                from_left = pltpu.roll(hrecv[1, n], (left_at - 29 - at) % 128, 1)
                from_right = pltpu.roll(hrecv[0, n], (right_at - at) % 128, 1)
                ref[left_row : left_row + CR] = jnp.where(
                    span(left_at), from_left, ref[left_row : left_row + CR]
                )
                ref[right_row : right_row + CR] = jnp.where(
                    span(right_at), from_right, ref[right_row : right_row + CR]
                )

    END = ROWS * (PAIRS + 1)
    sub_up = functools.partial(pltpu.roll, shift=1, axis=0)

    def sub_down(x):
        return pltpu.roll(x, x.shape[0] - 1, 0)

    def across(x):
        x0, x1, x2 = x[:CR], x[CR : 2 * CR], x[2 * CR :]
        return (
            jnp.where(lane16 < 53, pltpu.roll(x1, 72, 1), pltpu.roll(x2, 50, 1)),
            pltpu.roll(x2, 68, 1),
            pltpu.roll(x0, SPLIT, 1),
            jnp.where(lane16 < 63, pltpu.roll(x0, 78, 1), pltpu.roll(x1, 60, 1)),
        )

    def wrap(ref):
        a, b, c, d = across(ref[END - ROWS : END])
        ref[:CR] = sub_up(a)
        ref[CR : 2 * CR] = jnp.where(lane16 < SPLIT, sub_up(b), c)
        ref[2 * CR : ROWS] = d
        a, b, c, d = across(ref[ROWS : 2 * ROWS])
        ref[END : END + CR] = a
        ref[END + CR : END + 2 * CR] = jnp.where(lane16 < SPLIT, b, sub_down(c))
        ref[END + 2 * CR :] = sub_down(d)

    wrap(dirs)

    def finish(b, step):
        top, bottom = ROWS + HALO * ROWS, ROWS + ROWS + CR - 1
        for f in range(FIELDS):
            wrap(moving.at[b, f])
            enter[step, 0, f, 6:7] = moving[b, f, top : top + 1]
            enter[step, 0, f, 14:15] = moving[b, f, top + CR : top + CR + 1]
            enter[step, 1, f, 1:2] = moving[b, f, bottom + CR : bottom + CR + 1]
            enter[step, 1, f, 9:10] = moving[b, f, bottom + 2 * CR : bottom + 2 * CR + 1]

    def main_in(b, r, c):
        masks = inflow_masks(*[dirs[pl.ds(r + n * ROWS, CR), :] for n in range(3)])
        arriving = [
            inflow(masks, *[moving[b, f, pl.ds(r + n * ROWS, CR), :] for n in range(3)])
            for f in range(FIELDS)
        ]
        left = [rest[f, pl.ds(r, CR), :] for f in range(FIELDS)]
        return settle(left, arriving, [coarse[LAYERS + k, c : c + CR] for k in range(LAYERS)])

    def main_out(b, r, c, h, liquid):
        move, left, taken = outflow(
            h,
            liquid,
            stat[ORATE, pl.ds(r, CR), :],
            stat[LAND, pl.ds(r, CR), :],
            stat[CHANNEL, pl.ds(r, CR), :],
            stat[LRATE, pl.ds(r, CR), :],
            [coarse[k, c : c + CR] for k in range(LAYERS)],
            [coarse[2 * LAYERS + k, c : c + CR] for k in range(LAYERS)],
        )
        for f in range(FIELDS):
            moving[b, f, pl.ds(r + ROWS, CR), :] = move[f]
            rest[f, pl.ds(r, CR), :] = left[f]
        sums[LAYERS + 1, c : c + CR] += taken

    def row_at(p, c):
        return pl.multiple_of(p * ROWS + c, CR)

    sums[...] = jnp.zeros(sums.shape, jnp.float32)

    @pl.loop(0, PAIRS, unroll=True)
    def _(p):
        for c in range(0, ROWS, CR):
            r = row_at(p, c)
            h = coarse[4 * LAYERS, c : c + CR] * stat[SHARE, pl.ds(r, CR), :]
            main_out(0, r, c, h, [coarse[3 * LAYERS + k, c : c + CR] for k in range(LAYERS)])

    finish(0, 0)

    for b in range(2):

        @pl.loop(0, PAIRS, unroll=True)
        def _(p, b=b):
            for c in range(0, ROWS, CR):
                r = row_at(p, c)
                main_out(1 - b, r, c, *main_in(b, r, c))

        finish(1 - b, 1 + b)

    since = jnp.where(in_first, HALO, 0)
    until = jnp.where(in_last, PAIRS - HALO, PAIRS)

    @pl.loop(0, PAIRS, unroll=True)
    def _(p):
        for c in range(0, ROWS, CR):
            h, liquid = main_in(0, row_at(p, c), c)
            keep = (since[c : c + CR] <= p) & (until[c : c + CR] > p)
            for n, x in enumerate(liquid + [h]):
                sums[n, c : c + CR] += jnp.where(keep, x, 0.0)

    row_p, col_p = iota((128, 128), 0), iota((128, 128), 1)
    to_block = []
    for at, end, shift in ((3, 113, 0), (3, 53, 11), (3, 113, 5)):
        mine = (row_p >= at) & (row_p < end) & (tenth(row_p + 7) == col_p + 1 - shift)
        if shift == 11:
            mine = mine | ((row_p >= 59) & (row_p < 109) & (tenth(row_p - 49) == col_p + 1))
        to_block.append(jnp.where(mine, 1.0, 0.0).astype(jnp.bfloat16))
    to_block = jnp.concatenate(to_block, 0)
    scales = [0.01 / (1000.0 * x) for x in thickness] + [0.01, 0.01]

    def three(n):
        return jnp.concatenate([sums[n, c : c + CR] for c in range(0, ROWS, CR)], 1) * scales[n]

    means = dot2(jnp.concatenate([three(n) for n in range(LAYERS + 2)], 0), to_block)
    back = means[:CR]
    for n in range(1, LAYERS + 2):
        back = back + pltpu.roll(means[n * CR : (n + 1) * CR], 16 * n, 1)
    for s in range(1, CR - 1):
        bsend[s] = back[s : s + 1]

    def answer(k, s):
        return pltpu.make_async_remote_copy(
            src_ref=bsend.at[k],
            dst_ref=brecv.at[s],
            send_sem=bs_sem,
            recv_sem=br_sem,
            device_id=(mi, k),
            device_id_type=MESH,
        )

    def answers():
        return pltpu.make_async_remote_copy(
            src_ref=bsend.at[: nc - 1],
            dst_ref=brecv.at[: nc - 1],
            send_sem=bs_sem,
            recv_sem=br_sem,
            device_id=(mi, mj),
            device_id_type=MESH,
        )

    for k in others(mj):

        @pl.when((k != 0) & (k != nc - 1))
        def _(k=k):
            answer(k, mj).start()

    def strip(v):
        has, _, left, right, _ = sides[v]

        @pl.when(has)
        def _():
            vertical(1 - v, mi).wait_recv()
            piece(0, mi, CR + 1 - v, zh_sem, zr_sem.at[2 - v]).wait_recv()

        @pl.when(has & left)
        def _():
            corner(1 - v, 1, mi, mj).wait_recv()

        @pl.when(has & right)
        def _():
            corner(1 - v, 0, mi, mj).wait_recv()

        halo, far = vrecv.at[1 - v], (PAIRS if v else 0)
        for half, at in enumerate((SPLIT, 113) if v else (0, SPLIT - HALO)):
            index = jnp.clip(HALO * sub16 + lane16 - at, 0, 127)
            side = take(jnp.broadcast_to(crecv[1 - v, 1 - half], (CR, 128)), index)
            halo[half] = jnp.where(span(at), side, halo[half])
        for f in range(FIELDS):
            strip_own(f, v, sstat.at[f])
            for half in range(2):
                at = 8 * half + far
                sstat[f, at : at + HALO] = halo[half, HALO * f : HALO * f + HALO]

        sub = sub8 >= PAIRS if v else sub8 < HALO
        groups = [
            jnp.where(sub, zrecv[CR + 1 - v, :, at : at + 128], zrecv[v * (CR - 1), :, at : at + 128])
            for at in (0, 128)
        ]
        tables = columns(8)[v : v + 2]
        wide = [jnp.concatenate([take(groups[f // 5], c + 24 * (f % 5)) for c in tables], 0) for f in range(COARSE)]
        liquid, ice_w, room, per_pore = layers_of(wide)
        sdir = sstat[DIR]
        masks = inflow_masks(sub_up(sdir), sdir, sub_down(sdir))
        entering = (sub16 & 7) == (1 if v else 6)
        h = wide[0] * sstat[SHARE]
        channel = jnp.zeros((CR, 128), jnp.float32)
        for step in range(3):
            move, rest_s, taken = outflow(
                h, liquid, sstat[ORATE], sstat[LAND], schannel[v], sstat[LRATE], ice_w, per_pore
            )
            channel = channel + taken
            move = [jnp.where(entering, enter[step, v, f], m) for f, m in enumerate(move)]
            arriving = [inflow(masks, sub_up(m), m, sub_down(m)) for m in move]
            h, liquid = settle(rest_s, arriving, room)

        first_row = 2 if v else HALO
        mine = ((sub16 & 7) >= first_row) & ((sub16 & 7) < first_row + HALO)
        mine = mine & ((sub16 >= 8) | (lane16 >= SPLIT)) if v else mine & ((sub16 < 8) | (lane16 < SPLIT))
        rows = []
        for n, x in enumerate(liquid + [h, channel]):
            x = jnp.where(mine, x, 0.0) * scales[n]
            rows.append(jnp.concatenate([jnp.sum(x[at : at + 8], 0, keepdims=True) for at in (0, 8)], 1))
        rows.append(jnp.zeros((2, 2 * 128), jnp.float32))
        part = dot2(jnp.concatenate(rows, 0), to_block[128 * v : 128 * v + 256])
        part = pltpu.roll(part, 0, 1, stride=16, stride_axis=0)
        s = v * (CR - 1)
        bsend[s] = back[s : s + 1] + jnp.sum(part, 0, keepdims=True)

        @pl.when(mj != s)
        def _():
            answer(s, mj).start()

    lower_first = lax.rem(mi, 4) == 0

    @pl.when(lower_first)
    def _():
        strip(1)

    strip(0)

    @pl.when(jnp.logical_not(lower_first))
    def _():
        strip(1)

    brecv[mj] = bsend[mj]

    row_pieces().wait_send()

    @pl.when(first_up | last_down)
    def _():
        pltpu.make_async_remote_copy(
            src_ref=zsend,
            dst_ref=zrecv.at[:nc],
            send_sem=zh_sem,
            recv_sem=zr_sem.at[1],
            device_id=(mi, mj),
            device_id_type=MESH,
        ).wait_send()

    for v, (has, i, left, right, end) in enumerate(sides):

        @pl.when(has)
        def _(v=v, i=i):
            vertical(v, i).wait_send()

        @pl.when(has & left)
        def _(v=v, i=i):
            corner(v, 0, i, mj - 1).wait_send()

        @pl.when(has & right)
        def _(v=v, i=i):
            corner(v, 1, i, mj + 1).wait_send()

    @pl.when(has_left)
    def _():
        sideways(0, mj - 1).wait_send()

    @pl.when(has_right)
    def _():
        sideways(1, mj + 1).wait_send()

    answers().wait_recv()

    gather = jnp.minimum(iota((8, 128), 0) * 16 + (lane & 15), 127)
    owner = lax.shift_right_logical(lane, 4)
    for half in range(2):
        out = jnp.zeros((8, 128), jnp.float32)
        for s in range(8):
            x = jnp.broadcast_to(brecv[8 * half + s], (8, 128))
            out = jnp.where(owner == s, take(x, gather), out)
        lanes = slice(128 * half, 128 * half + 128)
        for k in range(LAYERS):
            out_liq[k, :, lanes] = out[k : k + 1]
        out_h[:, lanes] = out[LAYERS : LAYERS + 1]
        out_c[:, lanes] = out[LAYERS + 1 : LAYERS + 2]

    answers().wait_send()


def store(a, b, c, out_a, out_b, out_c, sem):
    copies = [
        pltpu.make_async_copy(src, dst, sem.at[n])
        for n, (src, dst) in enumerate(((a, out_a), (b, out_b), (c, out_c)))
    ]
    for copy in copies:
        copy.start()
    for copy in copies:
        copy.wait()


def solution(mesh):
    nr, nc = mesh.shape["rows"], mesh.shape["cols"]
    f32, bf16 = jnp.float32, jnp.bfloat16

    def step(*args):
        v = pltpu.VMEM
        dma = pltpu.SemaphoreType.DMA
        args = [pltpu.with_memory_space_constraint(x, pltpu.HBM) for x in args]
        results = pl.pallas_call(
            functools.partial(kernel, nr, nc),
            out_shape=(v((LAYERS, 1, W), f32), v((1, W), f32), v((1, W), f32)),
            in_specs=[pl.BlockSpec(memory_space=pltpu.HBM)] * 10,
            out_specs=[pl.BlockSpec(memory_space=pltpu.VMEM)] * 3,
            scratch_shapes=[
                v((1, W), f32),
                v((1, W), f32),
                v((1, W), f32),
                v((LAYERS, 1, W), f32),
                v((LAYERS, 1, W), f32),
                v((TILE, TILE), jnp.int32),
                v((TILE, TILE), jnp.int32),
                v((TILE, TILE), bf16),
                v((TILE, TILE), bf16),
                v((TILE, TILE), bf16),
                v((2 * FIELDS + 2, TILE, 128), f32),
                v((2 * REFINE, CR, 128), f32),
                v((FIELDS + 1, PAIRS * ROWS, 128), f32),
                v(((PAIRS + 2) * ROWS, 128), f32),
                v((4 * LAYERS + 1, ROWS, 128), f32),
                v((2, FIELDS, (PAIRS + 2) * ROWS, 128), f32),
                v((FIELDS, PAIRS * ROWS, 128), f32),
                v((LAYERS + 2, ROWS, 128), f32),
                v((FIELDS, CR, 128), f32),
                v((2, CR, 128), f32),
                v((3, 2, FIELDS, CR, 128), f32),
                v((CR, 1, W), f32),
                v((CR + 2, 1, W), f32),
                v((2, 2, CR, 128), f32),
                v((2, 2, CR, 128), f32),
                v((2, 2, 1, 128), f32),
                v((2, 2, 1, 128), f32),
                v((3, CR, 128), f32),
                v((2, 3, CR, 128), f32),
                v((CR, 1, 128), f32),
                v((CR, 1, 128), f32),
                dma((10,)),
                dma(()),
                dma(()),
                dma((3,)),
                dma((2,)),
                dma((2,)),
                dma((2, 2)),
                dma((2, 2)),
                dma((2,)),
                dma((2,)),
                dma(()),
                dma(()),
                pltpu.SemaphoreType.REGULAR,
                pltpu.SemaphoreType.REGULAR,
            ],
            compiler_params=pltpu.CompilerParams(
                collective_id=0, has_side_effects=True, vmem_limit_bytes=62 * 1024 * 1024
            ),
        )(*args)
        return pl.pallas_call(
            store,
            out_shape=(
                jax.ShapeDtypeStruct((LAYERS, 1, W), f32),
                jax.ShapeDtypeStruct((1, W), f32),
                jax.ShapeDtypeStruct((1, W), f32),
            ),
            in_specs=[pl.BlockSpec(memory_space=pltpu.VMEM)] * 3,
            out_specs=[pl.BlockSpec(memory_space=pltpu.HBM)] * 3,
            scratch_shapes=[dma((3,))],
        )(*[pltpu.with_memory_space_constraint(x, pltpu.VMEM) for x in results])

    return jax.shard_map(
        step,
        mesh=mesh,
        in_specs=(
            P(("rows", "cols"), None),
            P(("rows", "cols"), None),
            P(("rows", "cols"), None),
            P(None, ("rows", "cols"), None),
            P(None, ("rows", "cols"), None),
            P("rows", "cols"),
            P("rows", "cols"),
            P("rows", "cols"),
            P("rows", "cols"),
            P("rows", "cols"),
        ),
        out_specs=(
            P(None, ("rows", "cols"), None),
            P(("rows", "cols"), None),
            P(("rows", "cols"), None),
        ),
        check_vma=False,
    )
```

time: 20.7 us -> 19.5 us (0.942)
  Pallas kernels: 20 us -> 18.7 us
    pallas_call x1, Pallas kernels: 19.4 us -> 18.1 us  [step(): pl.pallas_call(functools.partial(kernel, nr, nc), out_shape=(v((LAYERS, 1...]
where the time goes in v3:
time: 19.5 us; the launch traced here: 19.4 us
  Pallas kernels  18.7 us (96%)
  between operations  0.64 us (3%)
    pallas_call x1, Pallas kernels, step(): pl.pallas_call(functools.partial(kernel, nr, nc), out_shape=(v((LAYERS, 1...  18.1 us
    pallas_call x1, Pallas kernels, step(): pl.pallas_call(store, out_shape=(jax.ShapeDtypeStruct((LAYERS, 1, W), f32...  0.63 us

profile of v3, /device:TPU:6, one launch (start us, length us, event | category | flops | bytes accessed | tf_op | source)
XLA Modules:
  0.0 19.4 jit_solution(6953147703189263399)
XLA Ops:
  0.6 18.1 %shard_map.121 = (f32[4,1,256]{2,1,0:T(1,128)S(1)}, f32[1,256]{1,0:T(1,128)S(1)}, f32[1,256]{1,0:T(1,128)S(1)}) custom-call(f32[1,256]{1,0:T(1,128)} %rain_h.1, f32[1,256]{1,0:T(1,128)} %infil_h.1, f32[1,256]{1,0:T(1,128)} %por_h.1, f32[4,1,256]{2,1,0:T(1,128)} %liq_h.1, f32[4,1,256]{2,1,0:T(1,128)} %ice_h.1, s32[160,160]{1,0:T(8,128)} %dir_h.1, ...), custom_call_target="tpu_custom_call" | custom-call | tf_op jit(solution)/shard_map/pallas_call | solution.py:927
  18.8 0.6 %shard_map.122 = (f32[4,1,256]{2,1,0:T(1,128)}, f32[1,256]{1,0:T(1,128)}, f32[1,256]{1,0:T(1,128)}) custom-call(f32[4,1,256]{2,1,0:T(1,128)S(1)} %get-tuple-element.6.a, f32[1,256]{1,0:T(1,128)S(1)} %get-tuple-element.7.b, f32[1,256]{1,0:T(1,128)S(1)} %get-tuple-element.8.c), custom_call_target="tpu_custom_call" | custom-call | tf_op jit(solution)/shard_map/pallas_call | solution.py:983

commit v4 on v3

--- a/solution.py
+++ b/solution.py
@@ -146,6 +146,8 @@
     orate_v,
     lrate_v,
     weight_v,
+    same_block_v,
+    to_block_v,
     nat,
     share_v,
     stat,
@@ -181,6 +183,7 @@
     br_sem,
     row_sem,
     relay_sem,
+    late_sem,
 ):
     mi = lax.axis_index("rows")
     mj = lax.axis_index("cols")
@@ -222,30 +225,63 @@
         (has_up, mi - 1, has_left, has_right, nc - 1),
         (has_down, mi + 1, has_left, has_right, 0),
     )
-    for has, i, left, right, end in sides:
-
-        @pl.when(has)
-        def _(i=i, end=end):
-            tell(i, end)
-
-        @pl.when(has & jnp.logical_not(is_lead))
-        def _(i=i):
-            tell(i, mj)
-
-        @pl.when(has & left & (mj - 1 != lead))
-        def _(i=i):
-            tell(i, mj - 1)
-
-        @pl.when(has & right & (mj + 1 != lead))
-        def _(i=i):
-            tell(i, mj + 1)
+    late = (lax.rem(mi, 4) == 3) & has_down
+    late_side = (has_up & (lax.rem(mi, 4) != 0), late)
+    early_side = (has_up & (lax.rem(mi, 4) == 0), has_down & (lax.rem(mi, 4) != 3))
+    own_end = (0, nc - 1)
+
+    def partners(v, signal):
+        has, i, left, right, end = sides[v]
+        signal(i, end)
+        signal(i, mj)
+
+        @pl.when(left)
+        def _():
+            signal(i, mj - 1)
+
+        @pl.when(right)
+        def _():
+            signal(i, mj + 1)
+
+        @pl.when(mj == own_end[v])
+        def _():
+            @pl.loop(0, nc)
+            def _(k):
+                signal(i, k)
+
+    def count(v):
+        one = 2 + has_left.astype(jnp.int32) + has_right.astype(jnp.int32)
+        return one + nc * (mj == own_end[v]).astype(jnp.int32)
+
+    def tell_late_one(i, j):
+        @pl.when(j != lead)
+        def _():
+            tell(i, j)
+
+    for v in range(2):
+
+        @pl.when(early_side[v])
+        def _(v=v):
+            partners(v, tell_late_one)
 
     @pl.when(is_lead)
     def _():
         pl.semaphore_wait(barrier, nc - 1)
-        for k in range(nc):
-            if k != lead:
-                pl.semaphore_signal(row_sem, inc=1, device_id=(mi, k), device_id_type=MESH)
+        near = [lead - 1, lead + 1]
+        for k in near + [k for k in others(lead) if k not in near]:
+            pl.semaphore_signal(row_sem, inc=1, device_id=(mi, k), device_id_type=MESH)
+
+    row_c, col_c = iota((W, W), 0), iota((W, W), 1)
+    same_block = (tenth(row_c) == tenth(col_c)) & (row_c < TILE) & (col_c < TILE)
+    same_block_v[...] = jnp.where(same_block, 1.0, 0.0).astype(jnp.bfloat16)
+    row_p, col_p = iota((128, 128), 0), iota((128, 128), 1)
+    to_block = []
+    for at, end, shift in ((3, 113, 0), (3, 53, 11), (3, 113, 5)):
+        mine = (row_p >= at) & (row_p < end) & (tenth(row_p + 7) == col_p + 1 - shift)
+        if shift == 11:
+            mine = mine | ((row_p >= 59) & (row_p < 109) & (tenth(row_p - 49) == col_p + 1))
+        to_block.append(jnp.where(mine, 1.0, 0.0).astype(jnp.bfloat16))
+    to_block_v[...] = jnp.concatenate(to_block, 0)
 
     lane = iota((8, 128), 1)
     lane16 = iota((CR, 128), 1)
@@ -312,51 +348,41 @@
             device_id_type=MESH,
         )
 
-    incoming = 0
-    for has, i, left, right, end in sides:
-        incoming += has.astype(jnp.int32) + (has & left).astype(jnp.int32) + (has & right).astype(jnp.int32)
-    incoming += nc * ((has_up & (mj == 0)).astype(jnp.int32) + (has_down & (mj == nc - 1)).astype(jnp.int32))
+    incoming = sum(late_side[v].astype(jnp.int32) * count(v) for v in range(2))
+
+    any_late = late_side[0] | late_side[1]
+    passes_on = (mj == lead - 1) | (mj == lead + 1)
 
     def rows_ready():
-        @pl.when(jnp.logical_not(is_lead))
-        def _():
-            pl.semaphore_wait(barrier, incoming)
-
-        @pl.when((mj == lead - 1) | (mj == lead + 1))
-        def _():
-            pl.semaphore_signal(relay_sem, inc=1, device_id=(mi, lead), device_id_type=MESH)
-
-        @pl.when(is_lead)
-        def _():
-            pl.semaphore_wait(relay_sem, 2)
-
-    def send_ends():
-        @pl.when(first_up)
+        pl.semaphore_wait(barrier, incoming)
+
+    def pass_on():
+        pl.semaphore_signal(relay_sem, inc=1, device_id=(mi, lead), device_id_type=MESH)
+
+    def send_ends(v):
+        @pl.when(mj == own_end[v])
         def _():
             @pl.loop(0, nc)
             def _(k):
-                piece(k, mi - 1, CR, zh_sem, zr_sem.at[1]).start()
-
-        @pl.when(last_down)
-        def _():
-            @pl.loop(0, nc)
-            def _(k):
-                piece(k, mi + 1, CR + 1, zh_sem, zr_sem.at[2]).start()
-
-    def send_rows():
-        for v, (has, i, left, right, end) in enumerate(sides):
-
-            @pl.when(has)
-            def _(v=v, i=i):
-                vertical(v, i).start()
-
-            @pl.when(has & left)
-            def _(v=v, i=i):
-                corner(v, 0, i, mj - 1).start()
-
-            @pl.when(has & right)
-            def _(v=v, i=i):
-                corner(v, 1, i, mj + 1).start()
+                piece(k, sides[v][1], CR + v, zh_sem, zr_sem.at[1 + v]).start()
+
+    def send_rows(v):
+        _, i, left, right, _ = sides[v]
+        vertical(v, i).start()
+
+        @pl.when(left)
+        def _():
+            corner(v, 0, i, mj - 1).start()
+
+        @pl.when(right)
+        def _():
+            corner(v, 1, i, mj + 1).start()
+
+    def tell_early(v):
+        def signal(i, j):
+            pl.semaphore_signal(late_sem.at[1 - v], inc=1, device_id=(i, j), device_id_type=MESH)
+
+        partners(v, signal)
 
     def coarse_part():
         for copy in copies[:5]:
@@ -395,9 +421,53 @@
         def _():
             zrecv[CR + 1] = zsend[mj]
 
-    def tile_part():
+    def tile_arrived():
         for copy in copies[5:]:
             copy.wait()
+
+    def vertical_part():
+        no_lanes = jnp.zeros((CR, 96), jnp.float32)
+
+        def in_halves(x):
+            return x[:, :128], jnp.concatenate([x[:, 128:], no_lanes[: x.shape[0]]], 1)
+
+        edges, totals = [], []
+        for v in range(2):
+            r = v * (TILE - CR)
+            kind_x = kind_v[r : r + CR]
+            edge = [
+                dir_v[r : r + CR].astype(jnp.float32),
+                jnp.where(kind_x == 2, 0.0, orate_v[r : r + CR].astype(jnp.float32)),
+                jnp.where(kind_x == 0, 1.0, 0.0),
+                lrate_v[r : r + CR].astype(jnp.float32),
+                weight_v[r : r + CR].astype(jnp.float32),
+            ]
+            edge = [in_halves(x) for x in edge]
+            mine = sub16 >= CR - REFINE if v else sub16 < REFINE
+            total = [jnp.sum(jnp.where(mine, x, 0.0), 0, keepdims=True) for x in edge[SHARE]]
+            edges.append(edge)
+            totals.append(jnp.concatenate(total, 1))
+        totals.append(jnp.zeros((6, W), jnp.float32))
+        per_mean = 100.0 / jnp.where(iota((8, W), 1) < TILE, dot3(jnp.concatenate(totals, 0), same_block_v[...]), 1.0)
+        place = lane16 - HALO * sub16
+        for v in (1, 0):
+            r = v * (CR - HALO)
+            for half in range(2):
+                scale = per_mean[v : v + 1, 128 * half : 128 * half + 128]
+                for f in range(FIELDS):
+                    x = edges[v][f][half][r : r + HALO]
+                    vsend[v, half, HALO * f : HALO * f + HALO] = x * scale if f == SHARE else x
+                vsend[v, half, HALO * FIELDS :] = jnp.zeros((1, 128), jnp.float32)
+            a, b = vsend[v, 0], vsend[v, 1]
+            if v == 0:
+                vsend[v, 0], vsend[v, 1] = third_run(a), fourth_run(a, b)
+            else:
+                vsend[v, 0], vsend[v, 1] = first_run(a), second_run(a, b)
+            for n, (x, at) in enumerate(((a, 0), (b, 29))):
+                end = jnp.where((place >= 0) & (place < HALO), take(x, jnp.clip(place + at, 0, 127)), 0.0)
+                csend[v, n] = jnp.sum(end, 0, keepdims=True)
+
+    def tile_part():
         kind_x = kind_v[...]
         natural = (
             dir_v[...].astype(jnp.float32),
@@ -414,66 +484,75 @@
 
         weights = [rows_of(SHARE, rr) for rr in range(REFINE)]
         total = [functools.reduce(lambda a, b: a + b, [w[half] for w in weights]) for half in range(2)]
-        row_c, col_c = iota((W, W), 0), iota((W, W), 1)
-        same_block = (tenth(row_c) == tenth(col_c)) & (row_c < TILE) & (col_c < TILE)
-        block_sum = dot3(jnp.concatenate(total, 1), jnp.where(same_block, 1.0, 0.0).astype(jnp.bfloat16))
+        block_sum = dot3(jnp.concatenate(total, 1), same_block_v[...])
         per_mean = 100.0 / jnp.where(iota((CR, W), 1) < TILE, block_sum, 1.0)
         shares = [[w[half] * per_mean[:, 128 * half : 128 * half + 128] for half in range(2)] for w in weights]
         for rr in range(REFINE):
             for half in range(2):
                 share_v[2 * rr + half] = shares[rr][half]
 
-        place = lane16 - HALO * sub16
-        for v in range(2):
-            r = v * (TILE - HALO)
-            for half in range(2):
-                for f in range(SHARE):
-                    vsend[v, half, HALO * f : HALO * f + HALO] = nat[2 * f + half, r : r + HALO]
-                for p in range(HALO):
-                    x = shares[p + v * (REFINE - HALO)][half][v * (CR - 1) : v * (CR - 1) + 1]
-                    vsend[v, half, HALO * SHARE + p : HALO * SHARE + p + 1] = x
-                vsend[v, half, HALO * FIELDS :] = jnp.zeros((1, 128), jnp.float32)
-            a, b = vsend[v, 0], vsend[v, 1]
-            if v == 0:
-                vsend[v, 0], vsend[v, 1] = third_run(a), fourth_run(a, b)
-            else:
-                vsend[v, 0], vsend[v, 1] = first_run(a), second_run(a, b)
-            for n, (x, at) in enumerate(((a, 0), (b, 29))):
-                end = jnp.where((place >= 0) & (place < HALO), take(x, jnp.clip(place + at, 0, 127)), 0.0)
-                csend[v, n] = jnp.sum(end, 0, keepdims=True)
-
-    late = (lax.rem(mi, 4) == 3) & has_down
-    late_first = late.astype(jnp.int32)
-
-    @pl.loop(0, 2)
-    def _(phase):
-        part = lax.rem(phase + late_first, 2)
-
-        @pl.when(part == 0)
-        def _():
-            coarse_part()
-
-        @pl.when(part == 1)
-        def _():
-            tile_part()
-
-        @pl.when((phase == 0) & jnp.logical_not(is_lead))
+    def send_pieces():
+        for k in others(mj):
+            piece(k, mi, mj, zs_sem, zr_sem.at[0]).start()
+
+    def meet_early():
+        @pl.when(passes_on)
         def _():
             pl.semaphore_wait(row_sem, 1)
 
-        @pl.when(part == 0)
-        def _():
-            for k in others(mj):
-                piece(k, mi, mj, zs_sem, zr_sem.at[0]).start()
-
-        @pl.when((part == 1) & late)
+        @pl.when(jnp.logical_not(is_lead))
         def _():
             rows_ready()
-            send_rows()
+
+        @pl.when(passes_on)
+        def _():
+            pass_on()
+
+        @pl.when(is_lead)
+        def _():
+            pl.semaphore_wait(relay_sem, 2)
+
+        for v in (1, 0):
+
+            @pl.when(late_side[v])
+            def _(v=v):
+                tell_early(v)
+
+    def send_late():
+        for v in (1, 0):
+
+            @pl.when(late_side[v])
+            def _(v=v):
+                send_rows(v)
 
     @pl.when(late)
     def _():
-        send_ends()
+        tile_arrived()
+        vertical_part()
+        meet_early()
+        send_late()
+
+    coarse_part()
+
+    @pl.when(late)
+    def _():
+        send_ends(1)
+        send_ends(0)
+
+    @pl.when(is_lead)
+    def _():
+        send_pieces()
+
+    @pl.when(jnp.logical_not(late))
+    def _():
+        tile_arrived()
+
+    tile_part()
+
+    @pl.when(any_late & jnp.logical_not(late))
+    def _():
+        meet_early()
+        send_ends(0)
 
     shares = [[share_v[2 * rr + half] for half in range(2)] for rr in range(REFINE)]
 
@@ -501,6 +580,14 @@
             device_id_type=MESH,
         )
 
+    @pl.when(jnp.logical_not(is_lead))
+    def _():
+        @pl.when(jnp.logical_not(any_late & passes_on))
+        def _():
+            pl.semaphore_wait(row_sem, 1)
+
+        send_pieces()
+
     @pl.when(has_left)
     def _():
         sideways(0, mj - 1).start()
@@ -508,6 +595,11 @@
     @pl.when(has_right)
     def _():
         sideways(1, mj + 1).start()
+
+    @pl.when(jnp.logical_not(late))
+    def _():
+        vertical_part()
+        send_late()
 
     for p in range(PAIRS):
         for f in range(FIELDS + 1):
@@ -541,11 +633,14 @@
         r = p * ROWS
         stat[CHANNEL, r : r + ROWS] = jnp.where(out, 0.0, stat[CHANNEL, r : r + ROWS])
 
-    @pl.when(jnp.logical_not(late))
-    def _():
-        rows_ready()
-        send_ends()
-        send_rows()
+    def send_early(v):
+        @pl.when(early_side[v])
+        def _():
+            pl.semaphore_wait(late_sem.at[v], count(v))
+            send_rows(v)
+            send_ends(v)
+
+    send_early(1)
 
     for v, (has, i, left, right, end) in enumerate(sides):
 
@@ -587,19 +682,6 @@
             room.append((por_w - wide[2 + LAYERS + k]) * depth)
             per_pore.append((math.sqrt(layer_speed[k]) / depth) / por_w)
         return liquid, ice_w, room, per_pore
-
-    row_pieces().wait_recv()
-
-    def rows_at(group, slots):
-        return jnp.concatenate([zrecv[n, :, 128 * group : 128 * group + 128] for n in slots], 0)
-
-    packed_rows = [rows_at(g, range(CR)) for g in range(2)]
-    wide = [
-        jnp.concatenate([take(packed_rows[f // 5], c + 24 * (f % 5)) for c in columns(CR)], 0) for f in range(COARSE)
-    ]
-    liquid_w, ice_w, room, per_pore = layers_of(wide)
-    for n, x in enumerate(ice_w + room + per_pore + liquid_w + wide[:1]):
-        coarse[n] = x
 
     @pl.when(has_right)
     def _():
@@ -656,6 +738,20 @@
         ref[END + 2 * CR :] = sub_down(d)
 
     wrap(dirs)
+    sums[...] = jnp.zeros(sums.shape, jnp.float32)
+
+    row_pieces().wait_recv()
+
+    def rows_at(group, slots):
+        return jnp.concatenate([zrecv[n, :, 128 * group : 128 * group + 128] for n in slots], 0)
+
+    packed_rows = [rows_at(g, range(CR)) for g in range(2)]
+    wide = [
+        jnp.concatenate([take(packed_rows[f // 5], c + 24 * (f % 5)) for c in columns(CR)], 0) for f in range(COARSE)
+    ]
+    liquid_w, ice_w, room, per_pore = layers_of(wide)
+    for n, x in enumerate(ice_w + room + per_pore + liquid_w + wide[:1]):
+        coarse[n] = x
 
     def finish(b, step):
         top, bottom = ROWS + HALO * ROWS, ROWS + ROWS + CR - 1
@@ -694,8 +790,6 @@
     def row_at(p, c):
         return pl.multiple_of(p * ROWS + c, CR)
 
-    sums[...] = jnp.zeros(sums.shape, jnp.float32)
-
     @pl.loop(0, PAIRS, unroll=True)
     def _(p):
         for c in range(0, ROWS, CR):
@@ -726,20 +820,12 @@
             for n, x in enumerate(liquid + [h]):
                 sums[n, c : c + CR] += jnp.where(keep, x, 0.0)
 
-    row_p, col_p = iota((128, 128), 0), iota((128, 128), 1)
-    to_block = []
-    for at, end, shift in ((3, 113, 0), (3, 53, 11), (3, 113, 5)):
-        mine = (row_p >= at) & (row_p < end) & (tenth(row_p + 7) == col_p + 1 - shift)
-        if shift == 11:
-            mine = mine | ((row_p >= 59) & (row_p < 109) & (tenth(row_p - 49) == col_p + 1))
-        to_block.append(jnp.where(mine, 1.0, 0.0).astype(jnp.bfloat16))
-    to_block = jnp.concatenate(to_block, 0)
     scales = [0.01 / (1000.0 * x) for x in thickness] + [0.01, 0.01]
 
     def three(n):
         return jnp.concatenate([sums[n, c : c + CR] for c in range(0, ROWS, CR)], 1) * scales[n]
 
-    means = dot2(jnp.concatenate([three(n) for n in range(LAYERS + 2)], 0), to_block)
+    means = dot2(jnp.concatenate([three(n) for n in range(LAYERS + 2)], 0), to_block_v[...])
     back = means[:CR]
     for n in range(1, LAYERS + 2):
         back = back + pltpu.roll(means[n * CR : (n + 1) * CR], 16 * n, 1)
@@ -829,7 +915,7 @@
             x = jnp.where(mine, x, 0.0) * scales[n]
             rows.append(jnp.concatenate([jnp.sum(x[at : at + 8], 0, keepdims=True) for at in (0, 8)], 1))
         rows.append(jnp.zeros((2, 2 * 128), jnp.float32))
-        part = dot2(jnp.concatenate(rows, 0), to_block[128 * v : 128 * v + 256])
+        part = dot2(jnp.concatenate(rows, 0), to_block_v[128 * v : 128 * v + 256])
         part = pltpu.roll(part, 0, 1, stride=16, stride_axis=0)
         s = v * (CR - 1)
         bsend[s] = back[s : s + 1] + jnp.sum(part, 0, keepdims=True)
@@ -839,6 +925,7 @@
             answer(s, mj).start()
 
     lower_first = lax.rem(mi, 4) == 0
+    send_early(0)
 
     @pl.when(lower_first)
     def _():
@@ -940,6 +1027,8 @@
                 v((TILE, TILE), bf16),
                 v((TILE, TILE), bf16),
                 v((TILE, TILE), bf16),
+                v((W, W), bf16),
+                v((3 * 128, 128), bf16),
                 v((2 * FIELDS + 2, TILE, 128), f32),
                 v((2 * REFINE, CR, 128), f32),
                 v((FIELDS + 1, PAIRS * ROWS, 128), f32),
@@ -975,6 +1064,7 @@
                 dma(()),
                 pltpu.SemaphoreType.REGULAR,
                 pltpu.SemaphoreType.REGULAR,
+                pltpu.SemaphoreType.REGULAR((2,)),
             ],
             compiler_params=pltpu.CompilerParams(
                 collective_id=0, has_side_effects=True, vmem_limit_bytes=62 * 1024 * 1024

time: 19.5 us -> 19.3 us (0.990)
  Pallas kernels: 18.7 us -> 18.5 us
    pallas_call x1, Pallas kernels: 18.1 us -> 17.9 us  [step(): pl.pallas_call(functools.partial(kernel, nr, nc), out_shape=(v((LAYERS, 1...]
where the time goes in v4:
time: 19.3 us; the launch traced here: 19.2 us
  Pallas kernels  18.5 us (96%)
  between operations  0.64 us (3%)
    pallas_call x1, Pallas kernels, step(): pl.pallas_call(functools.partial(kernel, nr, nc), out_shape=(v((LAYERS, 1...  17.9 us
    pallas_call x1, Pallas kernels, step(): pl.pallas_call(store, out_shape=(jax.ShapeDtypeStruct((LAYERS, 1, W), f32...  0.63 us

profile of v4, /device:TPU:6, one launch (start us, length us, event | category | flops | bytes accessed | tf_op | source)
XLA Modules:
  0.0 19.2 jit_solution(8509861035261353052)
XLA Ops:
  0.6 17.9 %shard_map.121 = (f32[4,1,256]{2,1,0:T(1,128)S(1)}, f32[1,256]{1,0:T(1,128)S(1)}, f32[1,256]{1,0:T(1,128)S(1)}) custom-call(f32[1,256]{1,0:T(1,128)} %rain_h.1, f32[1,256]{1,0:T(1,128)} %infil_h.1, f32[1,256]{1,0:T(1,128)} %por_h.1, f32[4,1,256]{2,1,0:T(1,128)} %liq_h.1, f32[4,1,256]{2,1,0:T(1,128)} %ice_h.1, s32[160,160]{1,0:T(8,128)} %dir_h.1, ...), custom_call_target="tpu_custom_call" | custom-call | tf_op jit(solution)/shard_map/pallas_call | solution.py:1014
  18.5 0.6 %shard_map.122 = (f32[4,1,256]{2,1,0:T(1,128)}, f32[1,256]{1,0:T(1,128)}, f32[1,256]{1,0:T(1,128)}) custom-call(f32[4,1,256]{2,1,0:T(1,128)S(1)} %get-tuple-element.6.a, f32[1,256]{1,0:T(1,128)S(1)} %get-tuple-element.7.b, f32[1,256]{1,0:T(1,128)S(1)} %get-tuple-element.8.c), custom_call_target="tpu_custom_call" | custom-call | tf_op jit(solution)/shard_map/pallas_call | solution.py:1073

commit v5 on v4

--- a/solution.py
+++ b/solution.py
@@ -16,6 +16,8 @@
 W = 256
 HALO = 3
 PAIRS = REFINE // 2
+INNER_FIRST = tuple(range(1, PAIRS - 1)) + (0, PAIRS - 1)
+OUTER_FIRST = (0, PAIRS - 1) + tuple(range(1, PAIRS - 1))
 ROWS = 3 * CR
 SPLIT = 56
 
@@ -788,37 +790,48 @@
         sums[LAYERS + 1, c : c + CR] += taken
 
     def row_at(p, c):
-        return pl.multiple_of(p * ROWS + c, CR)
-
-    @pl.loop(0, PAIRS, unroll=True)
-    def _(p):
-        for c in range(0, ROWS, CR):
+        return p * ROWS + c
+
+    for c in range(0, ROWS, CR):
+        liquid = [coarse[3 * LAYERS + k, c : c + CR] for k in range(LAYERS)]
+        drain = []
+        for k in range(LAYERS):
+            sat = (liquid[k] + coarse[k, c : c + CR]) * coarse[2 * LAYERS + k, c : c + CR]
+            sat = jnp.minimum(sat, math.sqrt(layer_speed[k]))
+            drain.append(liquid[k] * (sat * sat))
+        taken_c = jnp.zeros((CR, 128), jnp.float32)
+        for p in OUTER_FIRST:
             r = row_at(p, c)
-            h = coarse[4 * LAYERS, c : c + CR] * stat[SHARE, pl.ds(r, CR), :]
-            main_out(0, r, c, h, [coarse[3 * LAYERS + k, c : c + CR] for k in range(LAYERS)])
+            h = coarse[4 * LAYERS, c : c + CR] * stat[SHARE, r : r + CR]
+            q = stat[ORATE, r : r + CR] * h * (h / (h + 2.0))
+            moving[0, 0, r + ROWS : r + ROWS + CR] = q * stat[LAND, r : r + CR]
+            rest[0, r : r + CR] = h - q
+            taken_c = taken_c + q * stat[CHANNEL, r : r + CR]
+            for k in range(LAYERS):
+                lateral = stat[LRATE, r : r + CR] * drain[k]
+                moving[0, 1 + k, r + ROWS : r + ROWS + CR] = lateral
+                rest[1 + k, r : r + CR] = liquid[k] - lateral
+        sums[LAYERS + 1, c : c + CR] = taken_c
 
     finish(0, 0)
 
     for b in range(2):
 
-        @pl.loop(0, PAIRS, unroll=True)
-        def _(p, b=b):
+        for p in INNER_FIRST:
             for c in range(0, ROWS, CR):
                 r = row_at(p, c)
                 main_out(1 - b, r, c, *main_in(b, r, c))
 
         finish(1 - b, 1 + b)
 
-    since = jnp.where(in_first, HALO, 0)
-    until = jnp.where(in_last, PAIRS - HALO, PAIRS)
-
-    @pl.loop(0, PAIRS, unroll=True)
-    def _(p):
+    for p in INNER_FIRST:
         for c in range(0, ROWS, CR):
             h, liquid = main_in(0, row_at(p, c), c)
-            keep = (since[c : c + CR] <= p) & (until[c : c + CR] > p)
+            out = [in_first[c : c + CR]] * (p < HALO and c < 2 * CR) + [in_last[c : c + CR]] * (p >= PAIRS - HALO and c > 0)
             for n, x in enumerate(liquid + [h]):
-                sums[n, c : c + CR] += jnp.where(keep, x, 0.0)
+                for mine in out:
+                    x = jnp.where(mine, 0.0, x)
+                sums[n, c : c + CR] += x
 
     scales = [0.01 / (1000.0 * x) for x in thickness] + [0.01, 0.01]
 
@@ -860,6 +873,8 @@
 
     def strip(v):
         has, _, left, right, _ = sides[v]
+        for f in range(FIELDS):
+            strip_own(f, v, sstat.at[f])
 
         @pl.when(has)
         def _():
@@ -880,7 +895,6 @@
             side = take(jnp.broadcast_to(crecv[1 - v, 1 - half], (CR, 128)), index)
             halo[half] = jnp.where(span(at), side, halo[half])
         for f in range(FIELDS):
-            strip_own(f, v, sstat.at[f])
             for half in range(2):
                 at = 8 * half + far
                 sstat[f, at : at + HALO] = halo[half, HALO * f : HALO * f + HALO]
@@ -924,18 +938,9 @@
         def _():
             answer(s, mj).start()
 
-    lower_first = lax.rem(mi, 4) == 0
     send_early(0)
-
-    @pl.when(lower_first)
-    def _():
-        strip(1)
-
     strip(0)
-
-    @pl.when(jnp.logical_not(lower_first))
-    def _():
-        strip(1)
+    strip(1)
 
     brecv[mj] = bsend[mj]
 

time: 19.3 us -> 19.3 us (level)
  no operation moved by 1% of the time
where the time goes in v5:
time: 19.3 us; the launch traced here: 19.2 us
  Pallas kernels  18.5 us (96%)
  between operations  0.64 us (3%)
    pallas_call x1, Pallas kernels, step(): pl.pallas_call(functools.partial(kernel, nr, nc), out_shape=(v((LAYERS, 1...  17.9 us
    pallas_call x1, Pallas kernels, step(): pl.pallas_call(store, out_shape=(jax.ShapeDtypeStruct((LAYERS, 1, W), f32...  0.63 us

profile of v5, /device:TPU:6, one launch (start us, length us, event | category | flops | bytes accessed | tf_op | source)
XLA Modules:
  0.0 19.2 jit_solution(18405141189612090272)
XLA Ops:
  0.6 17.9 %shard_map.121 = (f32[4,1,256]{2,1,0:T(1,128)S(1)}, f32[1,256]{1,0:T(1,128)S(1)}, f32[1,256]{1,0:T(1,128)S(1)}) custom-call(f32[1,256]{1,0:T(1,128)} %rain_h.1, f32[1,256]{1,0:T(1,128)} %infil_h.1, f32[1,256]{1,0:T(1,128)} %por_h.1, f32[4,1,256]{2,1,0:T(1,128)} %liq_h.1, f32[4,1,256]{2,1,0:T(1,128)} %ice_h.1, s32[160,160]{1,0:T(8,128)} %dir_h.1, ...), custom_call_target="tpu_custom_call" | custom-call | tf_op jit(solution)/shard_map/pallas_call | solution.py:1019
  18.5 0.6 %shard_map.122 = (f32[4,1,256]{2,1,0:T(1,128)}, f32[1,256]{1,0:T(1,128)}, f32[1,256]{1,0:T(1,128)}) custom-call(f32[4,1,256]{2,1,0:T(1,128)S(1)} %get-tuple-element.6.a, f32[1,256]{1,0:T(1,128)S(1)} %get-tuple-element.7.b, f32[1,256]{1,0:T(1,128)S(1)} %get-tuple-element.8.c), custom_call_target="tpu_custom_call" | custom-call | tf_op jit(solution)/shard_map/pallas_call | solution.py:1078

commit v6 on v5

--- a/solution.py
+++ b/solution.py
@@ -737,7 +737,7 @@
         a, b, c, d = across(ref[ROWS : 2 * ROWS])
         ref[END : END + CR] = a
         ref[END + CR : END + 2 * CR] = jnp.where(lane16 < SPLIT, b, sub_down(c))
-        ref[END + 2 * CR :] = sub_down(d)
+        ref[END + 2 * CR : END + ROWS] = sub_down(d)
 
     wrap(dirs)
     sums[...] = jnp.zeros(sums.shape, jnp.float32)
@@ -1036,8 +1036,8 @@
                 v((3 * 128, 128), bf16),
                 v((2 * FIELDS + 2, TILE, 128), f32),
                 v((2 * REFINE, CR, 128), f32),
-                v((FIELDS + 1, PAIRS * ROWS, 128), f32),
-                v(((PAIRS + 2) * ROWS, 128), f32),
+                v((FIELDS + 1, 8 * ROWS, 128), f32),
+                v((9 * ROWS, 128), f32),
                 v((4 * LAYERS + 1, ROWS, 128), f32),
                 v((2, FIELDS, (PAIRS + 2) * ROWS, 128), f32),
                 v((FIELDS, PAIRS * ROWS, 128), f32),

time: 19.3 us -> 19.3 us (level)
  no operation moved by 1% of the time
where the time goes in v6:
time: 19.3 us; the launch traced here: 19.2 us
  Pallas kernels  18.5 us (96%)
  between operations  0.64 us (3%)
    pallas_call x1, Pallas kernels, step(): pl.pallas_call(functools.partial(kernel, nr, nc), out_shape=(v((LAYERS, 1...  17.9 us
    pallas_call x1, Pallas kernels, step(): pl.pallas_call(store, out_shape=(jax.ShapeDtypeStruct((LAYERS, 1, W), f32...  0.63 us

profile of v6, /device:TPU:6, one launch (start us, length us, event | category | flops | bytes accessed | tf_op | source)
XLA Modules:
  0.0 19.2 jit_solution(3822254914453512794)
XLA Ops:
  0.6 17.9 %shard_map.121 = (f32[4,1,256]{2,1,0:T(1,128)S(1)}, f32[1,256]{1,0:T(1,128)S(1)}, f32[1,256]{1,0:T(1,128)S(1)}) custom-call(f32[1,256]{1,0:T(1,128)} %rain_h.1, f32[1,256]{1,0:T(1,128)} %infil_h.1, f32[1,256]{1,0:T(1,128)} %por_h.1, f32[4,1,256]{2,1,0:T(1,128)} %liq_h.1, f32[4,1,256]{2,1,0:T(1,128)} %ice_h.1, s32[160,160]{1,0:T(8,128)} %dir_h.1, ...), custom_call_target="tpu_custom_call" | custom-call | tf_op jit(solution)/shard_map/pallas_call | solution.py:1019
  18.5 0.6 %shard_map.122 = (f32[4,1,256]{2,1,0:T(1,128)}, f32[1,256]{1,0:T(1,128)}, f32[1,256]{1,0:T(1,128)}) custom-call(f32[4,1,256]{2,1,0:T(1,128)S(1)} %get-tuple-element.6.a, f32[1,256]{1,0:T(1,128)S(1)} %get-tuple-element.7.b, f32[1,256]{1,0:T(1,128)S(1)} %get-tuple-element.8.c), custom_call_target="tpu_custom_call" | custom-call | tf_op jit(solution)/shard_map/pallas_call | solution.py:1078

commit v7 on v6

--- a/solution.py
+++ b/solution.py
@@ -865,11 +865,15 @@
             device_id_type=MESH,
         )
 
-    for k in others(mj):
-
-        @pl.when((k != 0) & (k != nc - 1))
-        def _(k=k):
-            answer(k, mj).start()
+    def inner(n):
+        return 1 + lax.rem(mj + n, CR - 2)
+
+    for n in (11, 3, 10, 2, 7, 6, 8, 9, 5, 4, 1, 0, 12):
+        answer(inner(n), mj).start()
+
+    @pl.when((mj == 0) | (mj == nc - 1))
+    def _():
+        answer(inner(CR - 3), mj).start()
 
     def strip(v):
         has, _, left, right, _ = sides[v]
@@ -938,8 +942,8 @@
         def _():
             answer(s, mj).start()
 
+    strip(0)
     send_early(0)
-    strip(0)
     strip(1)
 
     brecv[mj] = bsend[mj]

time: 19.3 us -> 19.3 us (level)
  no operation moved by 1% of the time
where the time goes in v7:
time: 19.3 us; the launch traced here: 19.2 us
  Pallas kernels  18.5 us (96%)
  between operations  0.64 us (3%)
    pallas_call x1, Pallas kernels, step(): pl.pallas_call(functools.partial(kernel, nr, nc), out_shape=(v((LAYERS, 1...  17.9 us
    pallas_call x1, Pallas kernels, step(): pl.pallas_call(store, out_shape=(jax.ShapeDtypeStruct((LAYERS, 1, W), f32...  0.63 us

profile of v7, /device:TPU:6, one launch (start us, length us, event | category | flops | bytes accessed | tf_op | source)
XLA Modules:
  0.0 19.2 jit_solution(3499769738806253835)
XLA Ops:
  0.6 17.9 %shard_map.121 = (f32[4,1,256]{2,1,0:T(1,128)S(1)}, f32[1,256]{1,0:T(1,128)S(1)}, f32[1,256]{1,0:T(1,128)S(1)}) custom-call(f32[1,256]{1,0:T(1,128)} %rain_h.1, f32[1,256]{1,0:T(1,128)} %infil_h.1, f32[1,256]{1,0:T(1,128)} %por_h.1, f32[4,1,256]{2,1,0:T(1,128)} %liq_h.1, f32[4,1,256]{2,1,0:T(1,128)} %ice_h.1, s32[160,160]{1,0:T(8,128)} %dir_h.1, ...), custom_call_target="tpu_custom_call" | custom-call | tf_op jit(solution)/shard_map/pallas_call | solution.py:1023
  18.5 0.6 %shard_map.122 = (f32[4,1,256]{2,1,0:T(1,128)}, f32[1,256]{1,0:T(1,128)}, f32[1,256]{1,0:T(1,128)}) custom-call(f32[4,1,256]{2,1,0:T(1,128)S(1)} %get-tuple-element.6.a, f32[1,256]{1,0:T(1,128)S(1)} %get-tuple-element.7.b, f32[1,256]{1,0:T(1,128)S(1)} %get-tuple-element.8.c), custom_call_target="tpu_custom_call" | custom-call | tf_op jit(solution)/shard_map/pallas_call | solution.py:1082

commit v8 on v7

--- a/solution.py
+++ b/solution.py
@@ -642,8 +642,6 @@
             send_rows(v)
             send_ends(v)
 
-    send_early(1)
-
     for v, (has, i, left, right, end) in enumerate(sides):
 
         @pl.when(jnp.logical_not(has))
@@ -742,6 +740,7 @@
     wrap(dirs)
     sums[...] = jnp.zeros(sums.shape, jnp.float32)
 
+    send_early(1)
     row_pieces().wait_recv()
 
     def rows_at(group, slots):

time: 19.3 us -> 19.3 us (level)
  no operation moved by 1% of the time
where the time goes in v8:
time: 19.3 us; the launch traced here: 19.2 us
  Pallas kernels  18.5 us (96%)
  between operations  0.64 us (3%)
    pallas_call x1, Pallas kernels, step(): pl.pallas_call(functools.partial(kernel, nr, nc), out_shape=(v((LAYERS, 1...  17.9 us
    pallas_call x1, Pallas kernels, step(): pl.pallas_call(store, out_shape=(jax.ShapeDtypeStruct((LAYERS, 1, W), f32...  0.63 us

profile of v8, /device:TPU:6, one launch (start us, length us, event | category | flops | bytes accessed | tf_op | source)
XLA Modules:
  0.0 19.2 jit_solution(13053822586379553549)
XLA Ops:
  0.6 17.9 %shard_map.121 = (f32[4,1,256]{2,1,0:T(1,128)S(1)}, f32[1,256]{1,0:T(1,128)S(1)}, f32[1,256]{1,0:T(1,128)S(1)}) custom-call(f32[1,256]{1,0:T(1,128)} %rain_h.1, f32[1,256]{1,0:T(1,128)} %infil_h.1, f32[1,256]{1,0:T(1,128)} %por_h.1, f32[4,1,256]{2,1,0:T(1,128)} %liq_h.1, f32[4,1,256]{2,1,0:T(1,128)} %ice_h.1, s32[160,160]{1,0:T(8,128)} %dir_h.1, ...), custom_call_target="tpu_custom_call" | custom-call | tf_op jit(solution)/shard_map/pallas_call | solution.py:1022
  18.5 0.6 %shard_map.122 = (f32[4,1,256]{2,1,0:T(1,128)}, f32[1,256]{1,0:T(1,128)}, f32[1,256]{1,0:T(1,128)}) custom-call(f32[4,1,256]{2,1,0:T(1,128)S(1)} %get-tuple-element.6.a, f32[1,256]{1,0:T(1,128)S(1)} %get-tuple-element.7.b, f32[1,256]{1,0:T(1,128)S(1)} %get-tuple-element.8.c), custom_call_target="tpu_custom_call" | custom-call | tf_op jit(solution)/shard_map/pallas_call | solution.py:1081
